TPU v7x, 512 devices: a whole 4x4x16 slice. The times are simulated.
512 devices in a mesh: grp: 16 (over y, x), slab: 32 (over z, core).
Axes of the slice: x: 4, y: 4, z: 16, core: 2. Of those that a mesh axis runs over, the one named last changes fastest.
Arguments:
- amplitudes: bfloat16 [2048, 16384], P('grp', 'slab'), may hold values from -6 to 6
- integrals: bfloat16 [128, 128, 16384], P('slab', None, 'grp'), may hold values from -0.109375 to 0.109375
- block_irrep: int32 [128], replicated, may hold values from 0 to 7
- slab_irrep: int32 [128], P('slab'), may hold values from 0 to 7
Outputs:
- ladder: bfloat16 [2048, 16384], P('grp', 'slab')
Inputs may be any that keep to these rules, and one draw needn't show every extreme that they name: `block_irrep`: pair irrep labels of the point group. `slab_irrep`: pair irrep labels of the point group.
All inputs are finite; a program needn't handle non-finite values.
Results may differ from a plain program's by a relative error of at most 0.001.
Values may be sent and summed in bfloat16 or wider, within the bound.
No kernel may reach another device: no remote copies, remote signals or barrier semaphores. Data moves between devices by JAX's collectives and lax.ppermute only.
A program may use at most 128 MiB of HBM per device.

v0:
```python
import jax
import jax.numpy as jnp
from jax import lax
from jax.sharding import PartitionSpec as P

BLK = 128


def block_gemm(rows, tile):
    return lax.dot_general(rows, tile, (((1,), (1,)), ((), ())), preferred_element_type=jnp.float32)


def local(amplitudes, integrals, block_irrep, slab_irrep):
    full_rows = lax.all_gather(amplitudes, "slab", axis=1, tiled=True)
    slabs, slab_rows, width = integrals.shape
    col_irrep = jnp.repeat(block_irrep, BLK)
    regrouped = lax.all_to_all(full_rows, "grp", split_axis=1, concat_axis=0, tiled=True)
    first_col = lax.axis_index("grp") * width
    labels = lax.dynamic_slice_in_dim(col_irrep, first_col, width, 0)
    keep = labels[None, :] == slab_irrep[:, None]
    masked = jnp.where(keep[:, None, :], integrals, jnp.zeros_like(integrals))
    masked = masked.reshape(slabs * slab_rows, width)
    summed = lax.psum_scatter(block_gemm(regrouped, masked), "grp", scatter_dimension=0, tiled=True)
    return summed.astype(jnp.bfloat16)


def solution(mesh):
    in_specs = (P("grp", "slab"), P("slab", None, "grp"), P(), P("slab"))
    out_specs = P("grp", "slab")
    return jax.shard_map(local, mesh=mesh, in_specs=in_specs, out_specs=out_specs, check_vma=False)
```

profile of v0, /device:TPU:1, one launch (start us, length us, event | category | flops | bytes accessed | tf_op | source)
XLA Modules:
  0.0 267.6 jit_solution(2865059309738734542)
XLA Ops:
  6.5 0.0 copy-start
  6.5 0.0 all-gather.2.cloned.1.call-start
  6.5 1.7 copy.7
  8.2 0.0 all-gather.2.cloned.1.call-update
  8.2 80.7 %all-gather.2.cloned.1.call-done = bf16[128,16384]{0,1:T(8,128)(2,1)} async-done(((bf16[128,512]{0,1:T(8,128)(2,1)}), bf16[128,16384]{0,1:T(8,128)(2,1)}) %all-gather.2.cloned.1.call-update) | async-done | bytes 4194320 | tf_op jit(solution)/shard_map/all_gather | solution.py:14
  89.0 0.0 copy-start.2
  89.0 0.0 copy-start.1
  89.0 7.0 %all-to-all-start = ((bf16[128,16,1024]{0,2,1:T(8,128)(2,1)}), bf16[128,16,1024]{0,2,1:T(8,128)(2,1)}, u32[]{:S(2)}, u32[]{:S(2)}) async-start(bf16[128,16,1024]{0,2,1:T(8,128)(2,1)} %bitcast.10), calls=%async_computation | async-start | bytes 8388608 | tf_op jit(solution)/shard_map/all_to_all | solution.py:17
  96.0 0.0 reduce-scatter.2.cloned.1.call-start
  96.1 0.0 copy-done
  96.1 0.1 broadcast_bitcast_fusion
  96.2 0.0 copy-done.2
  96.2 0.1 broadcast_compare_fusion
  96.3 0.0 copy-done.1
  96.3 0.1 broadcast_select_fusion
  96.4 62.5 %all-to-all-done = bf16[128,16,1024]{0,2,1:T(8,128)(2,1)} async-done(((bf16[128,16,1024]{0,2,1:T(8,128)(2,1)}), bf16[128,16,1024]{0,2,1:T(8,128)(2,1)}, u32[]{:S(2)}, u32[]{:S(2)}) %all-to-all-start) | async-done | bytes 4194336 | tf_op jit(solution)/shard_map/all_to_all | solution.py:17
  158.9 6.5 %copy.8 = bf16[16,128,1024]{2,1,0:T(8,128)(2,1)} copy(bf16[16,128,1024]{1,2,0:T(8,128)(2,1)} %bitcast.3) | data formatting | bytes 8388608 | tf_op jit(solution)/shard_map/all_to_all | solution.py:17
  165.4 6.5 %convolution_bitcast_fusion = f32[2048,512]{0,1:T(8,128)} fusion(bf16[512,1024]{1,0:T(8,128)(2,1)S(1)} %bitcast.12, bf16[2048,1024]{1,0:T(8,128)(2,1)} %bitcast.11), kind=kOutput, calls=%fused_computation | convolution fusion | flops 2147483648 | bytes 9437184 | tf_op jit(solution)/shard_map/dot_general | solution.py:10
  171.8 0.0 reduce-scatter.2.cloned.1.call-update
  171.9 87.2 %reduce-scatter.2.cloned.1.call-done = f32[128,512]{0,1:T(8,128)} async-done(((f32[2048,512]{0,1:T(8,128)}), f32[128,512]{0,1:T(8,128)}) %reduce-scatter.2.cloned.1.call-update) | async-done | bytes 262160 | tf_op jit(solution)/shard_map/reduce_scatter | solution.py:23
  259.1 1.0 convert_element_type.3
  260.0 0.8 copy.9
  (1 shorter events, 0.0 us)
Async XLA Ops:
  6.5 89.6 %copy-start = (s32[128]{0:T(128)S(1)}, s32[128]{0:T(128)}, u32[]{:S(2)}) copy-start(s32[128]{0:T(128)} %param.6) | copy-start | bytes 1540
  6.5 82.4 %all-gather.2.cloned.1.call-start = ((), (), s32[]{:S(2)}) async-start(), calls=%async_computation.2 | async-start | bytes 4325376 | tf_op jit(solution)/shard_map/all_gather | solution.py:14
  89.0 7.2 %copy-start.2 = (s32[4]{0:T(128)S(1)}, s32[4]{0:T(128)}, u32[]{:S(2)}) copy-start(s32[4]{0:T(128)} %param.7) | copy-start | bytes 52
  89.0 7.3 %copy-start.1 = (bf16[4,128,1024]{2,1,0:T(8,128)(2,1)S(1)}, bf16[4,128,1024]{2,1,0:T(8,128)(2,1)}, u32[]{:S(2)}) copy-start(bf16[4,128,1024]{2,1,0:T(8,128)(2,1)} %param.5) | copy-start | bytes 3145732
  89.0 69.9 %all-to-all-start = ((bf16[128,16,1024]{0,2,1:T(8,128)(2,1)}), bf16[128,16,1024]{0,2,1:T(8,128)(2,1)}, u32[]{:S(2)}, u32[]{:S(2)}) async-start(bf16[128,16,1024]{0,2,1:T(8,128)(2,1)} %bitcast.10), calls=%async_computation | async-start | bytes 8388608 | tf_op jit(solution)/shard_map/all_to_all | solution.py:17
  96.0 163.0 %reduce-scatter.2.cloned.1.call-start = ((), (), s32[]{:S(2)}) async-start(), calls=%async_computation.3 | async-start | bytes 4456448 | tf_op jit(solution)/shard_map/reduce_scatter | solution.py:23
Sparse Core Ops, SparseCore 0:
  9.5 79.4 all-gather.1
  172.0 87.0 reduce-scatter.1
where the time goes:
time: 269 us; the launch traced here: 268 us
  waiting for transfers between devices  231 us (86%)
  between operations  13.4 us (5%)
  local copies, waits for them, and re-layouts  8.99 us (3%)
  starting transfers between devices  7.08 us (3%)
  matrix products  6.5 us (2%)
    reduce_scatter x1, waiting for transfers between devices, local(): lax.psum_scatter(block_gemm(regrouped, masked), 'grp', scatter_dimension=...  87.2 us
    all_gather x1, waiting for transfers between devices, local(): full_rows = lax.all_gather(amplitudes, 'slab', axis=1, tiled=True)  80.7 us
    all_to_all x1, waiting for transfers between devices, local(): lax.all_to_all(full_rows, 'grp', split_axis=1, concat_axis=0, tiled=True)  62.5 us
    all_to_all x1, starting transfers between devices, local(): lax.all_to_all(full_rows, 'grp', split_axis=1, concat_axis=0, tiled=True)  7.03 us
    dot_general x1, matrix products, block_gemm(): lax.dot_general(rows, tile, (((1,), (1,)), ((), ())), preferred_element_t...  6.5 us
    all_to_all x1, local copies, waits for them, and re-layouts, local(): lax.all_to_all(full_rows, 'grp', split_axis=1, concat_axis=0, tiled=True)  6.45 us
  transfers between devices with their start and end apart: 3, of which 3 were waited for; matrix products, arithmetic and copies ran while one was open for 0% of the time, Pallas kernels for 0%

commit v1 on v0

v1 whole, which is shorter than its diff:
```python
import functools

import jax
import jax.numpy as jnp
import numpy as np
from jax import lax
from jax.experimental import pallas as pl
from jax.experimental.pallas import tpu as pltpu
from jax.sharding import Mesh, PartitionSpec as P

BLK = 128
NY, NX, NZ, NC = 4, 4, 16, 2
AXES = ("y", "x", "z", "c")


def moves(target):
    pairs = []
    for source in np.ndindex(NY, NX, NZ, NC):
        to = target(*source)
        pairs.append((int(np.ravel_multi_index(source, (NY, NX, NZ, NC))), int(np.ravel_multi_index(to, (NY, NX, NZ, NC)))))
    return pairs


def ring(size, step):
    return [(i, (i + step) % size) for i in range(size)]


def swap_cores(v):
    return lax.ppermute(v, "c", ring(NC, 1))


def class_gemm_kernel(where_ref, own, other, b0, b1, b2, b3, out):
    core, first = where_ref[0], where_ref[1]
    half = own.shape[2]
    total = jnp.zeros(out.shape, jnp.float32)
    for d, b in enumerate((b0, b1, b2, b3)):
        slot = lax.rem(first - d + 4, 4)
        mine, theirs = own[slot], other[slot]
        low = jnp.where(core == 0, mine, theirs)
        high = jnp.where(core == 0, theirs, mine)
        dims = (((1,), (1,)), ((), ()))
        total += lax.dot_general(low, b[:, :half], dims, preferred_element_type=jnp.float32)
        total += lax.dot_general(high, b[:, half:], dims, preferred_element_type=jnp.float32)
    out[...] = total


def class_gemm(where, own, other, bs):
    slots, rows, half = own.shape
    outs, width = bs[0].shape
    tile = outs // 2
    return pl.pallas_call(
        class_gemm_kernel,
        out_shape=jax.ShapeDtypeStruct((rows, outs), jnp.float32),
        grid_spec=pltpu.PrefetchScalarGridSpec(
            num_scalar_prefetch=1,
            grid=(outs // tile,),
            in_specs=[pl.BlockSpec((slots, rows, half), lambda n, w: (0, 0, 0))] * 2
            + [pl.BlockSpec((tile, width), lambda n, w: (n, 0))] * 4,
            out_specs=pl.BlockSpec((rows, tile), lambda n, w: (0, n)),
        ),
        compiler_params=pltpu.CompilerParams(vmem_limit_bytes=32 << 20),
        cost_estimate=pl.CostEstimate(flops=2 * rows * outs * width * 4, bytes_accessed=6 << 20, transcendentals=0),
    )(where, own, other, *bs)


def local(amplitudes, integrals, block_irrep, slab_irrep):
    y, x, z, c = (lax.axis_index(a) for a in AXES)
    slabs, slab_rows, width = integrals.shape

    parts = [
        lax.ppermute(
            amplitudes, AXES, moves(lambda y, x, z, c, j=j: (y, z % 4, (z + x - 1 + 4 * j) % NZ, c))
        )
        for j in range(4)
    ]

    labels = lax.dynamic_slice_in_dim(block_irrep, (y * NX + x) * (width // BLK), width // BLK, 0)
    keep = jnp.repeat(labels[None, :] == slab_irrep[:, None], BLK, axis=1)
    masked = jnp.where(keep[:, None, :], integrals, jnp.zeros_like(integrals)).reshape(slabs * slab_rows, width)
    bs = [masked] + [lax.ppermute(masked, "y", ring(NY, -d)) for d in range(1, 4)]

    here = jnp.stack(parts)
    classes = [(0, here)] + [(delta, lax.ppermute(here, "z", ring(NZ, -delta))) for delta in (1, -1, 2)]

    sums = []
    for delta, own in classes:
        other = swap_cores(own)
        plane = z + delta
        offset = lax.rem(plane - x + 1 + 2 * NZ, 4) - 1
        first = lax.rem(lax.rem(plane - offset + 2 * NZ, NZ) // 4 - y + 4, 4)
        where = jnp.stack([c, first]).astype(jnp.int32)
        part = class_gemm(where, own, other, bs)
        sums.append(
            lax.ppermute(
                part, AXES, moves(lambda y, x, z, c, delta=delta: (y, (z + delta - x + 1) % 4, z, c))
            )
        )
    return (sums[0] + sums[1] + sums[2] + sums[3]).astype(jnp.bfloat16)


def solution(mesh):
    split = Mesh(mesh.devices.reshape(NY, NX, NZ, NC), AXES)
    grp, slab = ("y", "x"), ("z", "c")
    in_specs = (P(grp, slab), P(slab, None, grp), P(), P(slab))
    return jax.shard_map(local, mesh=split, in_specs=in_specs, out_specs=P(grp, slab), check_vma=False)
```

time: 269 us -> 149 us (0.55)
  waiting for transfers between devices: 231 us -> 39.9 us
  starting transfers between devices: 7.08 us -> 87.5 us
  Pallas kernels: 0 us -> 14.3 us
  between operations: 13.4 us -> 0.39 us
  matrix products: 6.5 us -> 0 us
  local copies, waits for them, and re-layouts: 8.99 us -> 2.66 us
    ppermute x0 -> x18, starting transfers between devices: none -> 87.5 us  [the longest x4 28.8 us: local(): lax.ppermute(amplitudes, AXES, moves(lambda y, x, z, c, j=j: (y, z % 4, (...]
    reduce_scatter x1 -> x0, waiting for transfers between devices: 87.2 us -> none  [local(): lax.psum_scatter(block_gemm(regrouped, masked), 'grp', scatter_dimension=...]
    all_gather x1 -> x0, waiting for transfers between devices: 80.7 us -> none  [local(): full_rows = lax.all_gather(amplitudes, 'slab', axis=1, tiled=True)]
    all_to_all x1 -> x0, waiting for transfers between devices: 62.5 us -> none  [local(): lax.all_to_all(full_rows, 'grp', split_axis=1, concat_axis=0, tiled=True)]
    ppermute x0 -> x18, waiting for transfers between devices: none -> 39.9 us  [the longest x3 16.6 us: local(): lax.ppermute(here, 'z', ring(NZ, -delta))]
    pallas_call x0 -> x4, Pallas kernels: none -> 14.3 us  [class_gemm(): pl.pallas_call(class_gemm_kernel, out_shape=jax.ShapeDtypeStruct((rows, o...]
    all_to_all x1 -> x0, starting transfers between devices: 7.03 us -> none  [local(): lax.all_to_all(full_rows, 'grp', split_axis=1, concat_axis=0, tiled=True)]
    dot_general x1 -> x0, matrix products: 6.5 us -> none  [block_gemm(): lax.dot_general(rows, tile, (((1,), (1,)), ((), ())), preferred_element_t...]
  transfers between devices with their start and end apart: 3 -> 18, of which waited for: 3 -> 6; matrix products, arithmetic and copies ran while one was open for 0% -> 1% of each run, Pallas kernels for 0% -> 10%
where the time goes in v1:
time: 149 us; the launch traced here: 147 us
  starting transfers between devices  87.5 us (59%)
  waiting for transfers between devices  39.9 us (27%)
  Pallas kernels  14.3 us (10%)
  other arithmetic  2.72 us (2%)
  local copies, waits for them, and re-layouts  2.66 us (2%)
    ppermute x4, starting transfers between devices, local(): lax.ppermute(amplitudes, AXES, moves(lambda y, x, z, c, j=j: (y, z % 4, (...  28.8 us
    ppermute x4, starting transfers between devices, swap_cores(): return lax.ppermute(v, 'c', ring(NC, 1))  20.6 us
    ppermute x3, starting transfers between devices, local(): lax.ppermute(here, 'z', ring(NZ, -delta))  18.9 us
    ppermute x3, waiting for transfers between devices, local(): lax.ppermute(here, 'z', ring(NZ, -delta))  16.6 us
    pallas_call x4, Pallas kernels, class_gemm(): pl.pallas_call(class_gemm_kernel, out_shape=jax.ShapeDtypeStruct((rows, o...  14.3 us
    ppermute x4, waiting for transfers between devices, local(): lax.ppermute(amplitudes, AXES, moves(lambda y, x, z, c, j=j: (y, z % 4, (...  13.7 us
    ppermute x4, starting transfers between devices, local(): lax.ppermute(part, AXES, moves(lambda y, x, z, c, delta=delta: (y, (z + d...  9.66 us
    ppermute x3, starting transfers between devices, local(): lax.ppermute(masked, 'y', ring(NY, -d))  9.5 us
  transfers between devices with their start and end apart: 18, of which 6 were waited for; matrix products, arithmetic and copies ran while one was open for 1% of the time, Pallas kernels for 10%

profile of v1, /device:TPU:1, one launch (start us, length us, event | category | flops | bytes accessed | tf_op | source)
XLA Modules:
  0.0 147.4 jit_solution(3105088219700354842)
XLA Ops:
  0.0 15.1 %collective-permute-start.3 = (bf16[128,512]{1,0:T(8,128)(2,1)}, bf16[128,512]{1,0:T(8,128)(2,1)S(1)}, u32[]{:S(2)}, u32[]{:S(2)}) collective-permute-start(bf16[128,512]{1,0:T(8,128)(2,1)} %param.4), channel_id=1, source_target_pairs={{0,22},{1,23},{2,56},{3,57},{4,90},{5,91},{6,124},{7,125},{8,30},{... | collective-permute-start | bytes 393224 | tf_op jit(solution)/shard_map/ppermute | solution.py:71
  15.1 1.9 %collective-permute-start.2 = (bf16[128,512]{1,0:T(8,128)(2,1)}, bf16[128,512]{1,0:T(8,128)(2,1)S(1)}, u32[]{:S(2)}, u32[]{:S(2)}) collective-permute-start(bf16[128,512]{1,0:T(8,128)(2,1)} %param.4), channel_id=1, source_target_pairs={{0,14},{1,15},{2,48},{3,49},{4,82},{5,83},{6,116},{7,117},{8,22},{... | collective-permute-start | bytes 393224 | tf_op jit(solution)/shard_map/ppermute | solution.py:71
  17.0 8.1 %collective-permute-start.1 = (bf16[128,512]{1,0:T(8,128)(2,1)}, bf16[128,512]{1,0:T(8,128)(2,1)S(1)}, u32[]{:S(2)}, u32[]{:S(2)}) collective-permute-start(bf16[128,512]{1,0:T(8,128)(2,1)} %param.4), channel_id=1, source_target_pairs={{0,6},{1,7},{2,40},{3,41},{4,74},{5,75},{6,108},{7,109},{8,14},{9,... | collective-permute-start | bytes 393224 | tf_op jit(solution)/shard_map/ppermute | solution.py:71
  25.1 3.8 %collective-permute-start = (bf16[128,512]{1,0:T(8,128)(2,1)}, bf16[128,512]{1,0:T(8,128)(2,1)S(1)}, u32[]{:S(2)}, u32[]{:S(2)}) collective-permute-start(bf16[128,512]{1,0:T(8,128)(2,1)} %param.4), channel_id=1, source_target_pairs={{0,30},{1,31},{2,32},{3,33},{4,66},{5,67},{6,100},{7,101},{8,6},{9... | collective-permute-start | bytes 393224 | tf_op jit(solution)/shard_map/ppermute | solution.py:71
  28.9 0.7 dynamic_slice.3
  29.6 0.7 broadcast_compare_fusion
  30.3 0.1 broadcast_bitcast_fusion
  30.4 0.0 collective-permute-done.3
  30.4 4.8 %collective-permute-done.2 = bf16[128,512]{1,0:T(8,128)(2,1)S(1)} collective-permute-done((bf16[128,512]{1,0:T(8,128)(2,1)}, bf16[128,512]{1,0:T(8,128)(2,1)S(1)}, u32[]{:S(2)}, u32[]{:S(2)}) %collective-permute-start.2) | collective-permute-done | bytes 131104 | tf_op jit(solution)/shard_map/ppermute | solution.py:71
  35.2 9.0 %collective-permute-done.1 = bf16[128,512]{1,0:T(8,128)(2,1)S(1)} collective-permute-done((bf16[128,512]{1,0:T(8,128)(2,1)}, bf16[128,512]{1,0:T(8,128)(2,1)S(1)}, u32[]{:S(2)}, u32[]{:S(2)}) %collective-permute-start.1) | collective-permute-done | bytes 131104 | tf_op jit(solution)/shard_map/ppermute | solution.py:71
  44.2 0.9 pad_maximum_fusion.own
  45.0 12.3 %collective-permute-start.15 = (bf16[4,128,512]{2,1,0:T(8,128)(2,1)}, bf16[4,128,512]{2,1,0:T(8,128)(2,1)}, u32[]{:S(2)}, u32[]{:S(2)}) collective-permute-start(bf16[4,128,512]{2,1,0:T(8,128)(2,1)} %pad_maximum_fusion.own), channel_id=1, source_target_pairs={{0,28},{2,30},{4,0},{6,2},{8,4},{10,6},{12,8},{14,10},{16,12},{18,... | collective-permute-start | bytes 1572872 | tf_op jit(solution)/shard_map/ppermute | solution.py:83
  57.3 1.9 %collective-permute-start.12 = (bf16[4,128,512]{2,1,0:T(8,128)(2,1)}, bf16[4,128,512]{2,1,0:T(8,128)(2,1)}, u32[]{:S(2)}, u32[]{:S(2)}) collective-permute-start(bf16[4,128,512]{2,1,0:T(8,128)(2,1)} %pad_maximum_fusion.own), channel_id=1, source_target_pairs={{0,2},{2,4},{4,6},{6,8},{8,10},{10,12},{12,14},{14,16},{16,18},{18... | collective-permute-start | bytes 1572872 | tf_op jit(solution)/shard_map/ppermute | solution.py:83
  59.2 0.1 broadcast_select_fusion
  59.3 4.6 %collective-permute-start.5 = (bf16[512,1024]{1,0:T(8,128)(2,1)S(1)}, bf16[512,1024]{1,0:T(8,128)(2,1)S(1)}, u32[]{:S(2)}, u32[]{:S(2)}) collective-permute-start(bf16[512,1024]{1,0:T(8,128)(2,1)S(1)} %bitcast.15), channel_id=1, source_target_pairs={{0,384},{128,0},{256,128},{384,256},{1,385},{129,1},{257,129},{385... | collective-permute-start | bytes 3145736 | tf_op jit(solution)/shard_map/ppermute | solution.py:80
  64.0 2.3 %collective-permute-start.6 = (bf16[512,1024]{1,0:T(8,128)(2,1)S(1)}, bf16[512,1024]{1,0:T(8,128)(2,1)S(1)}, u32[]{:S(2)}, u32[]{:S(2)}) collective-permute-start(bf16[512,1024]{1,0:T(8,128)(2,1)S(1)} %bitcast.16), channel_id=1, source_target_pairs={{0,256},{128,384},{256,0},{384,128},{1,257},{129,385},{257,1},{385... | collective-permute-start | bytes 3145736 | tf_op jit(solution)/shard_map/ppermute | solution.py:80
  66.2 2.6 %collective-permute-start.7 = (bf16[512,1024]{1,0:T(8,128)(2,1)S(1)}, bf16[512,1024]{1,0:T(8,128)(2,1)}, u32[]{:S(2)}, u32[]{:S(2)}) collective-permute-start(bf16[512,1024]{1,0:T(8,128)(2,1)S(1)} %bitcast.17), channel_id=1, source_target_pairs={{0,128},{128,256},{256,384},{384,0},{1,129},{129,257},{257,385},{3... | collective-permute-start | bytes 3145736 | tf_op jit(solution)/shard_map/ppermute | solution.py:80
  68.9 8.0 %collective-permute-done.15.own = bf16[4,128,512]{2,1,0:T(8,128)(2,1)} collective-permute-done((bf16[4,128,512]{2,1,0:T(8,128)(2,1)}, bf16[4,128,512]{2,1,0:T(8,128)(2,1)}, u32[]{:S(2)}, u32[]{:S(2)}) %collective-permute-start.15) | collective-permute-done | bytes 524320 | tf_op jit(solution)/shard_map/ppermute | solution.py:83
  76.8 2.4 %collective-permute-start.4 = (bf16[4,128,512]{2,1,0:T(8,128)(2,1)}, bf16[4,128,512]{2,1,0:T(8,128)(2,1)S(1)}, u32[]{:S(2)}, u32[]{:S(2)}) collective-permute-start(bf16[4,128,512]{2,1,0:T(8,128)(2,1)} %pad_maximum_fusion.own), channel_id=1, source_target_pairs={{0,1},{1,0},{2,3},{3,2},{4,5},{5,4},{6,7},{7,6},{8,9},{9,8},{10,11... | collective-permute-start | bytes 1572872 | tf_op jit(solution)/shard_map/ppermute | solution.py:29
  79.3 0.0 collective-permute-done.12.own
  79.3 4.7 %collective-permute-start.9 = (bf16[4,128,512]{2,1,0:T(8,128)(2,1)}, bf16[4,128,512]{2,1,0:T(8,128)(2,1)}, u32[]{:S(2)}, u32[]{:S(2)}) collective-permute-start(bf16[4,128,512]{2,1,0:T(8,128)(2,1)} %pad_maximum_fusion.own), channel_id=1, source_target_pairs={{0,30},{2,0},{4,2},{6,4},{8,6},{10,8},{12,10},{14,12},{16,14},{18,... | collective-permute-start | bytes 1572872 | tf_op jit(solution)/shard_map/ppermute | solution.py:83
  84.0 0.0 collective-permute-done.4.other
  84.1 0.8 copy-done
  84.9 2.2 %collective-permute-start.16 = (bf16[4,128,512]{2,1,0:T(8,128)(2,1)}, bf16[4,128,512]{2,1,0:T(8,128)(2,1)}, u32[]{:S(2)}, u32[]{:S(2)}) collective-permute-start(bf16[4,128,512]{2,1,0:T(8,128)(2,1)} %collective-permute-done.15.own), channel_id=1, source_target_pairs={{0,1},{1,0},{2,3},{3,2},{4,5},{5,4},{6,7},{7,6},{8,9},{9,8},{10,11... | collective-permute-start | bytes 1572872 | tf_op jit(solution)/shard_map/ppermute | solution.py:29
  87.1 8.6 %collective-permute-done.9.own = bf16[4,128,512]{2,1,0:T(8,128)(2,1)} collective-permute-done((bf16[4,128,512]{2,1,0:T(8,128)(2,1)}, bf16[4,128,512]{2,1,0:T(8,128)(2,1)}, u32[]{:S(2)}, u32[]{:S(2)}) %collective-permute-start.9) | collective-permute-done | bytes 524320 | tf_op jit(solution)/shard_map/ppermute | solution.py:83
  95.7 2.7 %collective-permute-start.13 = (bf16[4,128,512]{2,1,0:T(8,128)(2,1)}, bf16[4,128,512]{2,1,0:T(8,128)(2,1)}, u32[]{:S(2)}, u32[]{:S(2)}) collective-permute-start(bf16[4,128,512]{2,1,0:T(8,128)(2,1)} %collective-permute-done.12.own), channel_id=1, source_target_pairs={{0,1},{1,0},{2,3},{3,2},{4,5},{5,4},{6,7},{7,6},{8,9},{9,8},{10,11... | collective-permute-start | bytes 1572872 | tf_op jit(solution)/shard_map/ppermute | solution.py:29
  98.4 0.0 collective-permute-done.5.b1
  98.4 13.3 %collective-permute-start.10 = (bf16[4,128,512]{2,1,0:T(8,128)(2,1)}, bf16[4,128,512]{2,1,0:T(8,128)(2,1)}, u32[]{:S(2)}, u32[]{:S(2)}) collective-permute-start(bf16[4,128,512]{2,1,0:T(8,128)(2,1)} %collective-permute-done.9.own), channel_id=1, source_target_pairs={{0,1},{1,0},{2,3},{3,2},{4,5},{5,4},{6,7},{7,6},{8,9},{9,8},{10,11... | collective-permute-start | bytes 1572872 | tf_op jit(solution)/shard_map/ppermute | solution.py:29
  111.7 0.1 pad_add_fusion.3.where_ref
  111.8 0.1 pad_add_fusion.2.where_ref
  111.9 0.1 pad_add_fusion.where_ref
  112.0 0.1 pad_add_fusion.1.where_ref
  112.1 3.0 %collective-permute-done.7.b3 = bf16[512,1024]{1,0:T(8,128)(2,1)} collective-permute-done((bf16[512,1024]{1,0:T(8,128)(2,1)S(1)}, bf16[512,1024]{1,0:T(8,128)(2,1)}, u32[]{:S(2)}, u32[]{:S(2)}) %collective-permute-start.7) | collective-permute-done | bytes 1048608 | tf_op jit(solution)/shard_map/ppermute | solution.py:80
  115.0 1.0 copy-done.1
  116.1 3.4 %shard_map.46 = f32[128,512]{1,0:T(8,128)S(1)} custom-call(s32[2]{0:T(128)S(1)} %pad_add_fusion.where_ref, bf16[4,128,512]{2,1,0:T(8,128)(2,1)} %pad_maximum_fusion.own, bf16[4,128,512]{2,1,0:T(8,128)(2,1)S(1)} %copy-done.1, bf16[512,1024]{1,0:T(8,128)(2,1)S(1)} %bitcast.18, bf16[512,1024]{1,0:T(8,128)(2,1)S(1)} %collective-permute-done.5.b1, ...), custom_call_target="tpu_custom_call" | custom-call | flops 536870912 | bytes 6291456 | tf_op jit(solution)/shard_map/pallas_call | solution.py:51
  119.5 3.4 %collective-permute-start.8 = (f32[128,512]{1,0:T(8,128)S(1)}, f32[128,512]{1,0:T(8,128)S(1)}, u32[]{:S(2)}, u32[]{:S(2)}) collective-permute-start(f32[128,512]{1,0:T(8,128)S(1)} %shard_map.46), channel_id=1, source_target_pairs={{0,32},{1,33},{2,66},{3,67},{4,100},{5,101},{6,6},{7,7},{8,40},{9,... | collective-permute-start | bytes 786440 | tf_op jit(solution)/shard_map/ppermute | solution.py:94
  122.9 0.0 collective-permute-done.16.other
  122.9 3.6 %shard_map.49 = f32[128,512]{1,0:T(8,128)S(1)} custom-call(s32[2]{0:T(128)S(1)} %pad_add_fusion.3.where_ref, bf16[4,128,512]{2,1,0:T(8,128)(2,1)} %collective-permute-done.15.own, bf16[4,128,512]{2,1,0:T(8,128)(2,1)} %collective-permute-done.16.other, bf16[512,1024]{1,0:T(8,128)(2,1)S(1)} %bitcast.19, bf16[512,1024]{1,0:T(8,128)(2,1)S(1)} %collective-permute-done.5.b1, ...), custom_call_target="tpu_custom_call" | custom-call | flops 536870912 | bytes 6291456 | tf_op jit(solution)/shard_map/pallas_call | solution.py:51
  126.5 1.9 %collective-permute-start.17 = (f32[128,512]{1,0:T(8,128)S(1)}, f32[128,512]{1,0:T(8,128)S(1)}, u32[]{:S(2)}, u32[]{:S(2)}) collective-permute-start(f32[128,512]{1,0:T(8,128)S(1)} %shard_map.49), channel_id=1, source_target_pairs={{0,96},{1,97},{2,2},{3,3},{4,36},{5,37},{6,70},{7,71},{8,104},{9,1... | collective-permute-start | bytes 786440 | tf_op jit(solution)/shard_map/ppermute | solution.py:94
  128.5 3.6 %shard_map.48 = f32[128,512]{1,0:T(8,128)S(1)} custom-call(s32[2]{0:T(128)S(1)} %pad_add_fusion.2.where_ref, bf16[4,128,512]{2,1,0:T(8,128)(2,1)} %collective-permute-done.12.own, bf16[4,128,512]{2,1,0:T(8,128)(2,1)} %collective-permute-done.13.other, bf16[512,1024]{1,0:T(8,128)(2,1)S(1)} %bitcast.20, bf16[512,1024]{1,0:T(8,128)(2,1)S(1)} %collective-permute-done.5.b1, ...), custom_call_target="tpu_custom_call" | custom-call | flops 536870912 | bytes 6291456 | tf_op jit(solution)/shard_map/pallas_call | solution.py:51
  132.1 0.7 collective-permute-start.14
  132.8 0.0 collective-permute-done.10.other
  132.8 3.6 %shard_map.47 = f32[128,512]{1,0:T(8,128)S(1)} custom-call(s32[2]{0:T(128)S(1)} %pad_add_fusion.1.where_ref, bf16[4,128,512]{2,1,0:T(8,128)(2,1)} %collective-permute-done.9.own, bf16[4,128,512]{2,1,0:T(8,128)(2,1)} %collective-permute-done.10.other, bf16[512,1024]{1,0:T(8,128)(2,1)S(1)} %bitcast.21, bf16[512,1024]{1,0:T(8,128)(2,1)S(1)} %collective-permute-done.5.b1, ...), custom_call_target="tpu_custom_call" | custom-call | flops 536870912 | bytes 6291456 | tf_op jit(solution)/shard_map/pallas_call | solution.py:51
  136.4 3.7 %collective-permute-start.11 = (f32[128,512]{1,0:T(8,128)S(1)}, f32[128,512]{1,0:T(8,128)S(1)}, u32[]{:S(2)}, u32[]{:S(2)}) collective-permute-start(f32[128,512]{1,0:T(8,128)S(1)} %shard_map.47), channel_id=1, source_target_pairs={{0,64},{1,65},{2,98},{3,99},{4,4},{5,5},{6,38},{7,39},{8,72},{9,73... | collective-permute-start | bytes 786440 | tf_op jit(solution)/shard_map/ppermute | solution.py:94
  140.1 0.0 collective-permute-done.17
  140.1 0.0 collective-permute-done.14
  140.1 6.6 %collective-permute-done.11 = f32[128,512]{1,0:T(8,128)S(1)} collective-permute-done((f32[128,512]{1,0:T(8,128)S(1)}, f32[128,512]{1,0:T(8,128)S(1)}, u32[]{:S(2)}, u32[]{:S(2)}) %collective-permute-start.11) | collective-permute-done | bytes 262176 | tf_op jit(solution)/shard_map/ppermute | solution.py:94
  146.7 0.7 add_convert_fusion
  (9 shorter events, 0.0 us)
Async XLA Ops:
  0.0 59.2 %copy-start.2 = (bf16[4,128,1024]{2,1,0:T(8,128)(2,1)S(1)}, bf16[4,128,1024]{2,1,0:T(8,128)(2,1)}, u32[]{:S(2)}) copy-start(bf16[4,128,1024]{2,1,0:T(8,128)(2,1)} %param.5) | copy-start | bytes 3145732
  0.0 30.4 %collective-permute-start.3 = (bf16[128,512]{1,0:T(8,128)(2,1)}, bf16[128,512]{1,0:T(8,128)(2,1)S(1)}, u32[]{:S(2)}, u32[]{:S(2)}) collective-permute-start(bf16[128,512]{1,0:T(8,128)(2,1)} %param.4), channel_id=1, source_target_pairs={{0,22},{1,23},{2,56},{3,57},{4,90},{5,91},{6,124},{7,125},{8,30},{... | collective-permute-start | bytes 393224 | tf_op jit(solution)/shard_map/ppermute | solution.py:71
  15.1 20.1 %collective-permute-start.2 = (bf16[128,512]{1,0:T(8,128)(2,1)}, bf16[128,512]{1,0:T(8,128)(2,1)S(1)}, u32[]{:S(2)}, u32[]{:S(2)}) collective-permute-start(bf16[128,512]{1,0:T(8,128)(2,1)} %param.4), channel_id=1, source_target_pairs={{0,14},{1,15},{2,48},{3,49},{4,82},{5,83},{6,116},{7,117},{8,22},{... | collective-permute-start | bytes 393224 | tf_op jit(solution)/shard_map/ppermute | solution.py:71
  17.0 27.2 %collective-permute-start.1 = (bf16[128,512]{1,0:T(8,128)(2,1)}, bf16[128,512]{1,0:T(8,128)(2,1)S(1)}, u32[]{:S(2)}, u32[]{:S(2)}) collective-permute-start(bf16[128,512]{1,0:T(8,128)(2,1)} %param.4), channel_id=1, source_target_pairs={{0,6},{1,7},{2,40},{3,41},{4,74},{5,75},{6,108},{7,109},{8,14},{9,... | collective-permute-start | bytes 393224 | tf_op jit(solution)/shard_map/ppermute | solution.py:71
  25.1 19.1 %collective-permute-start = (bf16[128,512]{1,0:T(8,128)(2,1)}, bf16[128,512]{1,0:T(8,128)(2,1)S(1)}, u32[]{:S(2)}, u32[]{:S(2)}) collective-permute-start(bf16[128,512]{1,0:T(8,128)(2,1)} %param.4), channel_id=1, source_target_pairs={{0,30},{1,31},{2,32},{3,33},{4,66},{5,67},{6,100},{7,101},{8,6},{9... | collective-permute-start | bytes 393224 | tf_op jit(solution)/shard_map/ppermute | solution.py:71
  45.0 31.8 %collective-permute-start.15 = (bf16[4,128,512]{2,1,0:T(8,128)(2,1)}, bf16[4,128,512]{2,1,0:T(8,128)(2,1)}, u32[]{:S(2)}, u32[]{:S(2)}) collective-permute-start(bf16[4,128,512]{2,1,0:T(8,128)(2,1)} %pad_maximum_fusion.own), channel_id=1, source_target_pairs={{0,28},{2,30},{4,0},{6,2},{8,4},{10,6},{12,8},{14,10},{16,12},{18,... | collective-permute-start | bytes 1572872 | tf_op jit(solution)/shard_map/ppermute | solution.py:83
  57.3 22.0 %collective-permute-start.12 = (bf16[4,128,512]{2,1,0:T(8,128)(2,1)}, bf16[4,128,512]{2,1,0:T(8,128)(2,1)}, u32[]{:S(2)}, u32[]{:S(2)}) collective-permute-start(bf16[4,128,512]{2,1,0:T(8,128)(2,1)} %pad_maximum_fusion.own), channel_id=1, source_target_pairs={{0,2},{2,4},{4,6},{6,8},{8,10},{10,12},{12,14},{14,16},{16,18},{18... | collective-permute-start | bytes 1572872 | tf_op jit(solution)/shard_map/ppermute | solution.py:83
  59.3 39.1 %collective-permute-start.5 = (bf16[512,1024]{1,0:T(8,128)(2,1)S(1)}, bf16[512,1024]{1,0:T(8,128)(2,1)S(1)}, u32[]{:S(2)}, u32[]{:S(2)}) collective-permute-start(bf16[512,1024]{1,0:T(8,128)(2,1)S(1)} %bitcast.15), channel_id=1, source_target_pairs={{0,384},{128,0},{256,128},{384,256},{1,385},{129,1},{257,129},{385... | collective-permute-start | bytes 3145736 | tf_op jit(solution)/shard_map/ppermute | solution.py:80
  64.0 48.1 %collective-permute-start.6 = (bf16[512,1024]{1,0:T(8,128)(2,1)S(1)}, bf16[512,1024]{1,0:T(8,128)(2,1)S(1)}, u32[]{:S(2)}, u32[]{:S(2)}) collective-permute-start(bf16[512,1024]{1,0:T(8,128)(2,1)S(1)} %bitcast.16), channel_id=1, source_target_pairs={{0,256},{128,384},{256,0},{384,128},{1,257},{129,385},{257,1},{385... | collective-permute-start | bytes 3145736 | tf_op jit(solution)/shard_map/ppermute | solution.py:80
  66.2 48.8 %collective-permute-start.7 = (bf16[512,1024]{1,0:T(8,128)(2,1)S(1)}, bf16[512,1024]{1,0:T(8,128)(2,1)}, u32[]{:S(2)}, u32[]{:S(2)}) collective-permute-start(bf16[512,1024]{1,0:T(8,128)(2,1)S(1)} %bitcast.17), channel_id=1, source_target_pairs={{0,128},{128,256},{256,384},{384,0},{1,129},{129,257},{257,385},{3... | collective-permute-start | bytes 3145736 | tf_op jit(solution)/shard_map/ppermute | solution.py:80
  76.8 7.2 %collective-permute-start.4 = (bf16[4,128,512]{2,1,0:T(8,128)(2,1)}, bf16[4,128,512]{2,1,0:T(8,128)(2,1)S(1)}, u32[]{:S(2)}, u32[]{:S(2)}) collective-permute-start(bf16[4,128,512]{2,1,0:T(8,128)(2,1)} %pad_maximum_fusion.own), channel_id=1, source_target_pairs={{0,1},{1,0},{2,3},{3,2},{4,5},{5,4},{6,7},{7,6},{8,9},{9,8},{10,11... | collective-permute-start | bytes 1572872 | tf_op jit(solution)/shard_map/ppermute | solution.py:29
  79.3 16.4 %collective-permute-start.9 = (bf16[4,128,512]{2,1,0:T(8,128)(2,1)}, bf16[4,128,512]{2,1,0:T(8,128)(2,1)}, u32[]{:S(2)}, u32[]{:S(2)}) collective-permute-start(bf16[4,128,512]{2,1,0:T(8,128)(2,1)} %pad_maximum_fusion.own), channel_id=1, source_target_pairs={{0,30},{2,0},{4,2},{6,4},{8,6},{10,8},{12,10},{14,12},{16,14},{18,... | collective-permute-start | bytes 1572872 | tf_op jit(solution)/shard_map/ppermute | solution.py:83
  84.1 0.8 copy-start
  84.9 38.0 %collective-permute-start.16 = (bf16[4,128,512]{2,1,0:T(8,128)(2,1)}, bf16[4,128,512]{2,1,0:T(8,128)(2,1)}, u32[]{:S(2)}, u32[]{:S(2)}) collective-permute-start(bf16[4,128,512]{2,1,0:T(8,128)(2,1)} %collective-permute-done.15.own), channel_id=1, source_target_pairs={{0,1},{1,0},{2,3},{3,2},{4,5},{5,4},{6,7},{7,6},{8,9},{9,8},{10,11... | collective-permute-start | bytes 1572872 | tf_op jit(solution)/shard_map/ppermute | solution.py:29
  95.7 32.8 %collective-permute-start.13 = (bf16[4,128,512]{2,1,0:T(8,128)(2,1)}, bf16[4,128,512]{2,1,0:T(8,128)(2,1)}, u32[]{:S(2)}, u32[]{:S(2)}) collective-permute-start(bf16[4,128,512]{2,1,0:T(8,128)(2,1)} %collective-permute-done.12.own), channel_id=1, source_target_pairs={{0,1},{1,0},{2,3},{3,2},{4,5},{5,4},{6,7},{7,6},{8,9},{9,8},{10,11... | collective-permute-start | bytes 1572872 | tf_op jit(solution)/shard_map/ppermute | solution.py:29
  98.4 34.4 %collective-permute-start.10 = (bf16[4,128,512]{2,1,0:T(8,128)(2,1)}, bf16[4,128,512]{2,1,0:T(8,128)(2,1)}, u32[]{:S(2)}, u32[]{:S(2)}) collective-permute-start(bf16[4,128,512]{2,1,0:T(8,128)(2,1)} %collective-permute-done.9.own), channel_id=1, source_target_pairs={{0,1},{1,0},{2,3},{3,2},{4,5},{5,4},{6,7},{7,6},{8,9},{9,8},{10,11... | collective-permute-start | bytes 1572872 | tf_op jit(solution)/shard_map/ppermute | solution.py:29
  115.0 1.0 copy-start.1
  119.5 20.6 %collective-permute-start.8 = (f32[128,512]{1,0:T(8,128)S(1)}, f32[128,512]{1,0:T(8,128)S(1)}, u32[]{:S(2)}, u32[]{:S(2)}) collective-permute-start(f32[128,512]{1,0:T(8,128)S(1)} %shard_map.46), channel_id=1, source_target_pairs={{0,32},{1,33},{2,66},{3,67},{4,100},{5,101},{6,6},{7,7},{8,40},{9,... | collective-permute-start | bytes 786440 | tf_op jit(solution)/shard_map/ppermute | solution.py:94
  126.5 13.6 %collective-permute-start.17 = (f32[128,512]{1,0:T(8,128)S(1)}, f32[128,512]{1,0:T(8,128)S(1)}, u32[]{:S(2)}, u32[]{:S(2)}) collective-permute-start(f32[128,512]{1,0:T(8,128)S(1)} %shard_map.49), channel_id=1, source_target_pairs={{0,96},{1,97},{2,2},{3,3},{4,36},{5,37},{6,70},{7,71},{8,104},{9,1... | collective-permute-start | bytes 786440 | tf_op jit(solution)/shard_map/ppermute | solution.py:94
  132.1 8.0 %collective-permute-start.14 = (f32[128,512]{1,0:T(8,128)S(1)}, f32[128,512]{1,0:T(8,128)S(1)}, u32[]{:S(2)}, u32[]{:S(2)}) collective-permute-start(f32[128,512]{1,0:T(8,128)S(1)} %shard_map.48), channel_id=1, source_target_pairs={{0,0},{1,1},{2,34},{3,35},{4,68},{5,69},{6,102},{7,103},{8,8},{9,9... | collective-permute-start | bytes 786440 | tf_op jit(solution)/shard_map/ppermute | solution.py:94
  136.4 10.3 %collective-permute-start.11 = (f32[128,512]{1,0:T(8,128)S(1)}, f32[128,512]{1,0:T(8,128)S(1)}, u32[]{:S(2)}, u32[]{:S(2)}) collective-permute-start(f32[128,512]{1,0:T(8,128)S(1)} %shard_map.47), channel_id=1, source_target_pairs={{0,64},{1,65},{2,98},{3,99},{4,4},{5,5},{6,38},{7,39},{8,72},{9,73... | collective-permute-start | bytes 786440 | tf_op jit(solution)/shard_map/ppermute | solution.py:94

commit v2 on v0

v2 whole, which is shorter than its diff:
```python
import jax
import jax.numpy as jnp
import numpy as np
from jax import lax
from jax.experimental import pallas as pl
from jax.experimental.pallas import tpu as pltpu
from jax.sharding import Mesh, PartitionSpec as P

BLK = 128
NY, NX, NZ, NC = 4, 4, 16, 2
AXES = ("y", "x", "z", "c")
FAR_PLANES = [[4 * zh + zl for zh in range(4)] for zl in range(4)]


def moves(target):
    pairs = []
    for source in np.ndindex(NY, NX, NZ, NC):
        to = target(*source)
        pairs.append((int(np.ravel_multi_index(source, (NY, NX, NZ, NC))), int(np.ravel_multi_index(to, (NY, NX, NZ, NC)))))
    return pairs


def spread(i):
    def target(y, x, z, c):
        step = (0, 1, 2 - 4 * c, -1)[(x + i) % 4]
        return (y, z % 4, (z + step) % NZ, c)

    return moves(target)


def gemm_kernel(info, *refs):
    own, other, b, out, total = refs[0:4], refs[4:8], refs[8], refs[9], refs[10]
    rows, half = own[0].shape[1:]
    core = info[0]
    mine = jnp.concatenate([r[0] for r in own])
    theirs = jnp.concatenate([r[0] for r in other])
    low = jnp.where(core == 0, mine, theirs)
    high = jnp.where(core == 0, theirs, mine)
    dims = (((1,), (1,)), ((), ()))
    part = lax.dot_general(low, b[0, :, :half], dims, preferred_element_type=jnp.float32)
    part += lax.dot_general(high, b[0, :, half:], dims, preferred_element_type=jnp.float32)

    @pl.when(pl.program_id(0) == 0)
    def _():
        total[...] = part

    @pl.when(pl.program_id(0) > 0)
    def _():
        total[...] += part

    @pl.when(pl.program_id(0) == 3)
    def _():
        for i in range(4):
            out[info[1 + i]] = total[i * rows : (i + 1) * rows]


def gemm(info, own, other, bs):
    slots, rows, half = own[0].shape
    _, outs, width = bs.shape
    piece = pl.BlockSpec((1, rows, half), lambda k, w: (k, 0, 0))
    return pl.pallas_call(
        gemm_kernel,
        out_shape=jax.ShapeDtypeStruct((4, rows, outs), jnp.float32),
        grid_spec=pltpu.PrefetchScalarGridSpec(
            num_scalar_prefetch=1,
            grid=(slots,),
            in_specs=[piece] * 8 + [pl.BlockSpec((1, outs, width), lambda k, w: (k, 0, 0))],
            out_specs=pl.BlockSpec((4, rows, outs), lambda k, w: (0, 0, 0)),
            scratch_shapes=[pltpu.VMEM((4 * rows, outs), jnp.float32)],
        ),
        compiler_params=pltpu.CompilerParams(vmem_limit_bytes=32 << 20),
        cost_estimate=pl.CostEstimate(
            flops=8 * rows * outs * width * slots, bytes_accessed=9 << 20, transcendentals=0
        ),
    )(info, *own, *other, bs)


def local(amplitudes, integrals, block_irrep, slab_irrep):
    y, x, z, c = (lax.axis_index(a) for a in AXES)
    slabs, slab_rows, width = integrals.shape

    labels = lax.dynamic_slice_in_dim(block_irrep, (y * NX + x) * (width // BLK), width // BLK, 0)
    keep = jnp.repeat(labels[None, :] == slab_irrep[:, None], BLK, axis=1)
    masked = jnp.where(keep[:, None, :], integrals, jnp.zeros_like(integrals)).reshape(slabs * slab_rows, width)
    bs = lax.all_gather(masked, "y", axis=0)

    here = lax.all_gather(amplitudes, "z", axis=0, axis_index_groups=FAR_PLANES)
    own = [lax.ppermute(here, AXES, spread(i)) for i in range(4)]
    other = [lax.ppermute(v, "c", [(0, 1), (1, 0)]) for v in own]

    places = [lax.rem(z - x - i + 8, 4) for i in range(4)]
    info = jnp.stack([c, *places]).astype(jnp.int32)
    parts = gemm(info, own, other, bs)
    parts = lax.all_to_all(parts, "x", split_axis=0, concat_axis=0)
    return parts.sum(0).astype(jnp.bfloat16)


def solution(mesh):
    split = Mesh(mesh.devices.reshape(NY, NX, NZ, NC), AXES)
    grp, slab = ("y", "x"), ("z", "c")
    in_specs = (P(grp, slab), P(slab, None, grp), P(), P(slab))
    return jax.shard_map(local, mesh=split, in_specs=in_specs, out_specs=P(grp, slab), check_vma=False)
```

time: 269 us -> 125 us (0.46)
  waiting for transfers between devices: 231 us -> 6.38 us
  blocking collectives: 0 us -> 57.1 us
  starting transfers between devices: 7.08 us -> 35.7 us
  matrix products: 6.5 us -> 0 us
  local copies, waits for them, and re-layouts: 8.99 us -> 3.09 us
  Pallas kernels: 0 us -> 5.15 us
    reduce_scatter x1 -> x0, waiting for transfers between devices: 87.2 us -> none  [local(): lax.psum_scatter(block_gemm(regrouped, masked), 'grp', scatter_dimension=...]
    all_gather x1, waiting for transfers between devices: 80.7 us -> 0.01 us  [local(): bs = lax.all_gather(masked, 'y', axis=0)]
    all_to_all x1 -> x0, waiting for transfers between devices: 62.5 us -> none  [local(): lax.all_to_all(full_rows, 'grp', split_axis=1, concat_axis=0, tiled=True)]
    ppermute x0 -> x8, starting transfers between devices: none -> 35.7 us  [the longest x4 21.4 us: local(): other = [lax.ppermute(v, 'c', [(0, 1), (1, 0)]) for v in own]]
    all_gather x0 -> x1, blocking collectives: none -> 31.4 us  [local(): here = lax.all_gather(amplitudes, 'z', axis=0, axis_index_groups=FAR_PLANES)]
    all_to_all x0 -> x1, blocking collectives: none -> 25.7 us  [local(): parts = lax.all_to_all(parts, 'x', split_axis=0, concat_axis=0)]
    all_to_all x1 -> x0, starting transfers between devices: 7.03 us -> none  [local(): lax.all_to_all(full_rows, 'grp', split_axis=1, concat_axis=0, tiled=True)]
    dot_general x1 -> x0, matrix products: 6.5 us -> none  [block_gemm(): lax.dot_general(rows, tile, (((1,), (1,)), ((), ())), preferred_element_t...]
  transfers between devices with their start and end apart: 3 -> 9, of which waited for: 3 -> 2; matrix products, arithmetic and copies ran while one was open for 0% -> 0% of each run, Pallas kernels for 0% -> 0%
where the time goes in v2:
time: 125 us
  blocking collectives  57.1 us (46%)
  starting transfers between devices  35.7 us (29%)
  between operations  13.5 us (11%)
  waiting for transfers between devices  6.38 us (5%)
  Pallas kernels  5.15 us (4%)
  other arithmetic  3.75 us (3%)
  local copies, waits for them, and re-layouts  3.09 us (2%)
    all_gather x1, blocking collectives, local(): here = lax.all_gather(amplitudes, 'z', axis=0, axis_index_groups=FAR_PLANES)  31.4 us
    all_to_all x1, blocking collectives, local(): parts = lax.all_to_all(parts, 'x', split_axis=0, concat_axis=0)  25.7 us
    ppermute x4, starting transfers between devices, local(): other = [lax.ppermute(v, 'c', [(0, 1), (1, 0)]) for v in own]  21.4 us
    ppermute x4, starting transfers between devices, local(): own = [lax.ppermute(here, AXES, spread(i)) for i in range(4)]  14.3 us
    pallas_call x1, Pallas kernels, gemm(): pl.pallas_call(gemm_kernel, out_shape=jax.ShapeDtypeStruct((4, rows, outs...  5.15 us
    ppermute x4, waiting for transfers between devices, local(): own = [lax.ppermute(here, AXES, spread(i)) for i in range(4)]  4.46 us
  transfers between devices with their start and end apart: 9, of which 2 were waited for; matrix products, arithmetic and copies ran while one was open for 0% of the time, Pallas kernels for 0%

profile of v2, /device:TPU:1, one launch (start us, length us, event | category | flops | bytes accessed | tf_op | source)
XLA Modules:
  0.0 124.7 jit_solution(17770609293326914575)
XLA Ops:
  6.5 0.0 all-gather.3.cloned.1.call-start
  6.5 0.7 dynamic_slice.3
  7.3 0.7 broadcast_compare_fusion
  8.0 0.1 broadcast_bitcast_fusion
  8.1 2.3 %broadcast_select_fusion = bf16[4,128,1024]{2,1,0:T(8,128)(2,1)} fusion(bf16[4,128,1024]{2,1,0:T(8,128)(2,1)} %param.5, pred[4,1024]{1,0:T(4,128)(4,1)S(1)} %bitcast.17), kind=kLoop, calls=%fused_computation | loop fusion | flops 524288 | bytes 2101248 | tf_op jit(solution)/shard_map/jit(_where)/select_n | solution.py:84
  10.3 0.0 all-gather.3.cloned.1.call-update
  10.4 31.4 %all-gather = bf16[512,512]{1,0:T(8,128)(2,1)S(1)} all-gather(bf16[128,512]{1,0:T(8,128)(2,1)} %param.4), channel_id=2, replica_groups={{0,8,16,24},{2,10,18,26},{4,12,20,28},{6,14,22,30},{1,9,17,25},{3,11,19..., dimensions={0}, use_global_device_ids=true | all-gather | bytes 655360 | tf_op jit(solution)/shard_map/all_gather | solution.py:87
  41.8 0.7 collective-permute-start
  42.5 4.9 %collective-permute-start.1 = (bf16[4,128,512]{2,1,0:T(8,128)(2,1)S(1)}, bf16[4,128,512]{2,1,0:T(8,128)(2,1)S(1)}, u32[]{:S(2)}, u32[]{:S(2)}) collective-permute-start(bf16[4,128,512]{2,1,0:T(8,128)(2,1)S(1)} %bitcast.14), channel_id=1, source_target_pairs={{0,2},{1,3},{2,36},{3,37},{4,70},{5,71},{6,104},{7,105},{8,10},{9,... | collective-permute-start | bytes 1572872 | tf_op jit(solution)/shard_map/ppermute | solution.py:88
  47.4 6.8 %collective-permute-start.2 = (bf16[4,128,512]{2,1,0:T(8,128)(2,1)S(1)}, bf16[4,128,512]{2,1,0:T(8,128)(2,1)S(1)}, u32[]{:S(2)}, u32[]{:S(2)}) collective-permute-start(bf16[4,128,512]{2,1,0:T(8,128)(2,1)S(1)} %bitcast.15), channel_id=1, source_target_pairs={{0,4},{1,29},{2,38},{3,63},{4,72},{5,65},{6,106},{7,99},{8,12},{9,... | collective-permute-start | bytes 1572872 | tf_op jit(solution)/shard_map/ppermute | solution.py:88
  54.2 1.9 %collective-permute-start.3 = (bf16[4,128,512]{2,1,0:T(8,128)(2,1)S(1)}, bf16[4,128,512]{2,1,0:T(8,128)(2,1)S(1)}, u32[]{:S(2)}, u32[]{:S(2)}) collective-permute-start(bf16[4,128,512]{2,1,0:T(8,128)(2,1)S(1)} %bitcast.16), channel_id=1, source_target_pairs={{0,30},{1,31},{2,32},{3,33},{4,66},{5,67},{6,100},{7,101},{8,6},{9... | collective-permute-start | bytes 1572872 | tf_op jit(solution)/shard_map/ppermute | solution.py:88
  56.1 0.0 collective-permute-done.refs_0_
  56.1 7.7 %collective-permute-start.4 = (bf16[4,128,512]{2,1,0:T(8,128)(2,1)S(1)}, bf16[4,128,512]{2,1,0:T(8,128)(2,1)S(1)}, u32[]{:S(2)}, u32[]{:S(2)}) collective-permute-start(bf16[4,128,512]{2,1,0:T(8,128)(2,1)S(1)} %collective-permute-done.refs_0_), channel_id=1, source_target_pairs={{0,1},{1,0},{2,3},{3,2},{4,5},{5,4},{6,7},{7,6},{8,9},{9,8},{10,11... | collective-permute-start | bytes 1572872 | tf_op jit(solution)/shard_map/ppermute | solution.py:89
  63.8 4.4 %collective-permute-done.1.refs_1_ = bf16[4,128,512]{2,1,0:T(8,128)(2,1)S(1)} collective-permute-done((bf16[4,128,512]{2,1,0:T(8,128)(2,1)S(1)}, bf16[4,128,512]{2,1,0:T(8,128)(2,1)S(1)}, u32[]{:S(2)}, u32[]{:S(2)}) %collective-permute-start.1) | collective-permute-done | bytes 524320 | tf_op jit(solution)/shard_map/ppermute | solution.py:88
  68.3 7.0 %collective-permute-start.5 = (bf16[4,128,512]{2,1,0:T(8,128)(2,1)S(1)}, bf16[4,128,512]{2,1,0:T(8,128)(2,1)S(1)}, u32[]{:S(2)}, u32[]{:S(2)}) collective-permute-start(bf16[4,128,512]{2,1,0:T(8,128)(2,1)S(1)} %collective-permute-done.1.refs_1_), channel_id=1, source_target_pairs={{0,1},{1,0},{2,3},{3,2},{4,5},{5,4},{6,7},{7,6},{8,9},{9,8},{10,11... | collective-permute-start | bytes 1572872 | tf_op jit(solution)/shard_map/ppermute | solution.py:89
  75.3 0.0 collective-permute-done.2.refs_2_
  75.3 4.8 %collective-permute-start.6 = (bf16[4,128,512]{2,1,0:T(8,128)(2,1)S(1)}, bf16[4,128,512]{2,1,0:T(8,128)(2,1)}, u32[]{:S(2)}, u32[]{:S(2)}) collective-permute-start(bf16[4,128,512]{2,1,0:T(8,128)(2,1)S(1)} %collective-permute-done.2.refs_2_), channel_id=1, source_target_pairs={{0,1},{1,0},{2,3},{3,2},{4,5},{5,4},{6,7},{7,6},{8,9},{9,8},{10,11... | collective-permute-start | bytes 1572872 | tf_op jit(solution)/shard_map/ppermute | solution.py:89
  80.1 0.0 collective-permute-done.3.refs_3_
  80.1 1.9 %collective-permute-start.7 = (bf16[4,128,512]{2,1,0:T(8,128)(2,1)S(1)}, bf16[4,128,512]{2,1,0:T(8,128)(2,1)}, u32[]{:S(2)}, u32[]{:S(2)}) collective-permute-start(bf16[4,128,512]{2,1,0:T(8,128)(2,1)S(1)} %collective-permute-done.3.refs_3_), channel_id=1, source_target_pairs={{0,1},{1,0},{2,3},{3,2},{4,5},{5,4},{6,7},{7,6},{8,9},{9,8},{10,11... | collective-permute-start | bytes 1572872 | tf_op jit(solution)/shard_map/ppermute | solution.py:89
  82.0 0.1 stack.23.info
  82.1 0.0 collective-permute-done.4.refs_4_
  82.1 0.0 collective-permute-done.5.refs_5_
  82.1 0.0 collective-permute-done.6.refs_6_
  82.1 1.9 %collective-permute-done.7.refs_7_ = bf16[4,128,512]{2,1,0:T(8,128)(2,1)} collective-permute-done((bf16[4,128,512]{2,1,0:T(8,128)(2,1)S(1)}, bf16[4,128,512]{2,1,0:T(8,128)(2,1)}, u32[]{:S(2)}, u32[]{:S(2)}) %collective-permute-start.7) | collective-permute-done | bytes 524320 | tf_op jit(solution)/shard_map/ppermute | solution.py:89
  84.0 0.0 all-gather.3.cloned.1.call-done.refs_8_
  84.0 0.0 copy-start
  84.0 2.2 %copy-done = bf16[4,512,1024]{2,1,0:T(8,128)(2,1)S(1)} copy-done((bf16[4,512,1024]{2,1,0:T(8,128)(2,1)S(1)}, bf16[4,512,1024]{2,1,0:T(8,128)(2,1)}, u32[]{:S(2)}) %copy-start) | copy-done | bytes 4194328
  86.2 5.1 %shard_map.46 = f32[4,128,512]{2,1,0:T(8,128)S(1)} custom-call(s32[5]{0:T(128)S(1)} %stack.23.info, bf16[4,128,512]{2,1,0:T(8,128)(2,1)S(1)} %collective-permute-done.refs_0_, bf16[4,128,512]{2,1,0:T(8,128)(2,1)S(1)} %collective-permute-done.1.refs_1_, bf16[4,128,512]{2,1,0:T(8,128)(2,1)S(1)} %collective-permute-done.2.refs_2_, ...), custom_call_target="tpu_custom_call" | custom-call | flops 2147483648 | bytes 9437184 | tf_op jit(solution)/shard_map/pallas_call | solution.py:61
  91.4 25.7 %all_to_all.5 = f32[4,128,512]{2,1,0:T(8,128)S(1)} all-to-all(f32[4,128,512]{2,1,0:T(8,128)S(1)} %shard_map.46), channel_id=1, replica_groups=mesh['y'=4,'x'=4,'z'=16,'c'=2] {'x'}, dimensions={0} | all-to-all | bytes 2097152 | tf_op jit(solution)/shard_map/all_to_all | solution.py:94
  117.1 0.8 reduce_sum.9
  (1 shorter events, 0.0 us)
Async XLA Ops:
  6.5 77.5 %all-gather.3.cloned.1.call-start = ((), (), s32[]{:S(2)}) async-start(), calls=%async_computation.1 | async-start | bytes 5242880 | tf_op jit(solution)/shard_map/all_gather | solution.py:85
  41.8 14.4 %collective-permute-start = (bf16[4,128,512]{2,1,0:T(8,128)(2,1)S(1)}, bf16[4,128,512]{2,1,0:T(8,128)(2,1)S(1)}, u32[]{:S(2)}, u32[]{:S(2)}) collective-permute-start(bf16[4,128,512]{2,1,0:T(8,128)(2,1)S(1)} %bitcast.13), channel_id=1, source_target_pairs={{0,0},{1,1},{2,34},{3,35},{4,68},{5,69},{6,102},{7,103},{8,8},{9,9... | collective-permute-start | bytes 1572872 | tf_op jit(solution)/shard_map/ppermute | solution.py:88
  42.5 25.8 %collective-permute-start.1 = (bf16[4,128,512]{2,1,0:T(8,128)(2,1)S(1)}, bf16[4,128,512]{2,1,0:T(8,128)(2,1)S(1)}, u32[]{:S(2)}, u32[]{:S(2)}) collective-permute-start(bf16[4,128,512]{2,1,0:T(8,128)(2,1)S(1)} %bitcast.14), channel_id=1, source_target_pairs={{0,2},{1,3},{2,36},{3,37},{4,70},{5,71},{6,104},{7,105},{8,10},{9,... | collective-permute-start | bytes 1572872 | tf_op jit(solution)/shard_map/ppermute | solution.py:88
  47.4 27.9 %collective-permute-start.2 = (bf16[4,128,512]{2,1,0:T(8,128)(2,1)S(1)}, bf16[4,128,512]{2,1,0:T(8,128)(2,1)S(1)}, u32[]{:S(2)}, u32[]{:S(2)}) collective-permute-start(bf16[4,128,512]{2,1,0:T(8,128)(2,1)S(1)} %bitcast.15), channel_id=1, source_target_pairs={{0,4},{1,29},{2,38},{3,63},{4,72},{5,65},{6,106},{7,99},{8,12},{9,... | collective-permute-start | bytes 1572872 | tf_op jit(solution)/shard_map/ppermute | solution.py:88
  54.2 25.9 %collective-permute-start.3 = (bf16[4,128,512]{2,1,0:T(8,128)(2,1)S(1)}, bf16[4,128,512]{2,1,0:T(8,128)(2,1)S(1)}, u32[]{:S(2)}, u32[]{:S(2)}) collective-permute-start(bf16[4,128,512]{2,1,0:T(8,128)(2,1)S(1)} %bitcast.16), channel_id=1, source_target_pairs={{0,30},{1,31},{2,32},{3,33},{4,66},{5,67},{6,100},{7,101},{8,6},{9... | collective-permute-start | bytes 1572872 | tf_op jit(solution)/shard_map/ppermute | solution.py:88
  56.1 26.0 %collective-permute-start.4 = (bf16[4,128,512]{2,1,0:T(8,128)(2,1)S(1)}, bf16[4,128,512]{2,1,0:T(8,128)(2,1)S(1)}, u32[]{:S(2)}, u32[]{:S(2)}) collective-permute-start(bf16[4,128,512]{2,1,0:T(8,128)(2,1)S(1)} %collective-permute-done.refs_0_), channel_id=1, source_target_pairs={{0,1},{1,0},{2,3},{3,2},{4,5},{5,4},{6,7},{7,6},{8,9},{9,8},{10,11... | collective-permute-start | bytes 1572872 | tf_op jit(solution)/shard_map/ppermute | solution.py:89
  68.3 13.9 %collective-permute-start.5 = (bf16[4,128,512]{2,1,0:T(8,128)(2,1)S(1)}, bf16[4,128,512]{2,1,0:T(8,128)(2,1)S(1)}, u32[]{:S(2)}, u32[]{:S(2)}) collective-permute-start(bf16[4,128,512]{2,1,0:T(8,128)(2,1)S(1)} %collective-permute-done.1.refs_1_), channel_id=1, source_target_pairs={{0,1},{1,0},{2,3},{3,2},{4,5},{5,4},{6,7},{7,6},{8,9},{9,8},{10,11... | collective-permute-start | bytes 1572872 | tf_op jit(solution)/shard_map/ppermute | solution.py:89
  75.3 6.8 %collective-permute-start.6 = (bf16[4,128,512]{2,1,0:T(8,128)(2,1)S(1)}, bf16[4,128,512]{2,1,0:T(8,128)(2,1)}, u32[]{:S(2)}, u32[]{:S(2)}) collective-permute-start(bf16[4,128,512]{2,1,0:T(8,128)(2,1)S(1)} %collective-permute-done.2.refs_2_), channel_id=1, source_target_pairs={{0,1},{1,0},{2,3},{3,2},{4,5},{5,4},{6,7},{7,6},{8,9},{9,8},{10,11... | collective-permute-start | bytes 1572872 | tf_op jit(solution)/shard_map/ppermute | solution.py:89
  80.1 3.9 %collective-permute-start.7 = (bf16[4,128,512]{2,1,0:T(8,128)(2,1)S(1)}, bf16[4,128,512]{2,1,0:T(8,128)(2,1)}, u32[]{:S(2)}, u32[]{:S(2)}) collective-permute-start(bf16[4,128,512]{2,1,0:T(8,128)(2,1)S(1)} %collective-permute-done.3.refs_3_), channel_id=1, source_target_pairs={{0,1},{1,0},{2,3},{3,2},{4,5},{5,4},{6,7},{7,6},{8,9},{9,8},{10,11... | collective-permute-start | bytes 1572872 | tf_op jit(solution)/shard_map/ppermute | solution.py:89
  84.0 2.2 %copy-start = (bf16[4,512,1024]{2,1,0:T(8,128)(2,1)S(1)}, bf16[4,512,1024]{2,1,0:T(8,128)(2,1)}, u32[]{:S(2)}) copy-start(bf16[4,512,1024]{2,1,0:T(8,128)(2,1)} %all-gather.3.cloned.1.call-done.refs_8_) | copy-start | bytes 12582916
Sparse Core Ops, SparseCore 0:
  10.5 61.2 all-gather.2

commit v3 on v0

v3 whole, which is shorter than its diff:
```python
import functools

import jax
import jax.numpy as jnp
import numpy as np
from jax import lax
from jax.experimental import pallas as pl
from jax.experimental.pallas import tpu as pltpu
from jax.sharding import Mesh, PartitionSpec as P

BLK = 128
NY, NX, NZ, NC = 4, 4, 16, 2
AXES = ("y", "x", "z", "c")
FAR_PLANES = [[4 * zh + zl for zh in range(4)] for zl in range(4)]


def moves(target):
    pairs = []
    for source in np.ndindex(NY, NX, NZ, NC):
        to = target(*source)
        pairs.append((int(np.ravel_multi_index(source, (NY, NX, NZ, NC))), int(np.ravel_multi_index(to, (NY, NX, NZ, NC)))))
    return pairs


def ring(size, step):
    return [(i, (i + step) % size) for i in range(size)]


def spread(k):
    def target(y, x, z, c):
        step = (0, 1, 2 if z % 2 == 0 else -2, -1)[(x - 2 * z + 2 * c + k) % 4]
        return (y, z % 4, (z + step) % NZ, c)

    return moves(target)


def home(k, cross):
    return moves(lambda y, x, z, c: (y, (z + x - 2 * c - k) % 4, z, c ^ cross))


def matched(b, info, blocks_at, start, count):
    return jnp.concatenate(
        [
            jnp.concatenate(
                [
                    jnp.where(
                        info[blocks_at + k] == info[2 + s],
                        b[s * BLK : (s + 1) * BLK, k * BLK : (k + 1) * BLK],
                        jnp.zeros((BLK, BLK), b.dtype),
                    )
                    for k in range(start, start + count)
                ],
                axis=1,
            )
            for s in range(b.shape[0] // BLK)
        ]
    )


def product(info, a, bs):
    slabs, blocks = bs[0].shape[0] // BLK, bs[0].shape[1] // BLK
    total = None
    for d, b in enumerate(bs):
        slot = lax.rem(info[1] + d, NY)
        for half in range(2):
            part = lax.dot_general(
                jnp.concatenate([r[half, slot] for r in a]),
                matched(b, info, 2 + slabs + slot * blocks, half * blocks // 2, blocks // 2),
                (((1,), (1,)), ((), ())),
                preferred_element_type=jnp.float32,
            )
            total = part if total is None else total + part
    return total


def gemm_kernel(info, a0, a1, b0, b1, b2, b3, out0, out1):
    total = product(info, (a0, a1), (b0, b1, b2, b3))
    rows = out0.shape[0]
    out0[...] = total[:rows]
    out1[...] = total[rows:]


def gemm(info, a, bs):
    _, slots, rows, half = a[0].shape
    columns, width = bs[0].shape
    smem, vmem = pl.BlockSpec(memory_space=pltpu.SMEM), pl.BlockSpec(memory_space=pltpu.VMEM)
    return pl.pallas_call(
        gemm_kernel,
        out_shape=[jax.ShapeDtypeStruct((rows, columns), jnp.float32)] * 2,
        in_specs=[smem] + [vmem] * 6,
        out_specs=[vmem] * 2,
        compiler_params=pltpu.CompilerParams(vmem_limit_bytes=16 << 20),
        cost_estimate=pl.CostEstimate(
            flops=4 * rows * columns * width * slots, bytes_accessed=6 << 20, transcendentals=0
        ),
    )(info, *a, *bs)


def local(amplitudes, integrals, block_irrep, slab_irrep):
    y, x, c = (lax.axis_index(a) for a in ("y", "x", "c"))
    slabs, slab_rows, width = integrals.shape

    b0 = integrals.reshape(slabs * slab_rows, width)
    b1 = lax.ppermute(b0, "y", ring(NY, -1))
    b3 = lax.ppermute(b0, "y", ring(NY, 1))

    here = lax.all_gather(amplitudes, "z", axis=0, axis_index_groups=FAR_PLANES)
    here, b0, b1, b3 = lax.optimization_barrier((here, b0, b1, b3))
    b2 = lax.ppermute(b0, "y", ring(NY, 2))
    there = lax.ppermute(here, "c", ring(NC, 1))
    both = jnp.where(c == 0, jnp.stack([here, there]), jnp.stack([there, here]))

    a = [lax.ppermute(both, AXES, spread(k)) for k in range(2)]

    bs = [b0, b1, b2, b3]
    peer_bs = [lax.ppermute(b, "c", ring(NC, 1)) for b in bs]
    peer_irrep = lax.ppermute(slab_irrep, "c", ring(NC, 1))
    column_irreps = lax.dynamic_index_in_dim(block_irrep.reshape(NY, NX, width // BLK), x, 1, keepdims=False)
    place = jnp.stack([c, y]).astype(jnp.int32)
    info, peer_info = (
        jnp.concatenate([place, irreps, column_irreps.reshape(-1)]) for irreps in (slab_irrep, peer_irrep)
    )

    sums = [lax.ppermute(part, AXES, home(k, 0)) for k, part in enumerate(gemm(info, a, bs))]
    sums += [lax.ppermute(part, AXES, home(k, 1)) for k, part in enumerate(gemm(peer_info, a, peer_bs))]
    return (sums[0] + sums[1] + sums[2] + sums[3]).astype(jnp.bfloat16)


def solution(mesh):
    split = Mesh(mesh.devices.reshape(NY, NX, NZ, NC), AXES)
    grp, slab = ("y", "x"), ("z", "c")
    in_specs = (P(grp, slab), P(slab, None, grp), P(), P(slab))
    return jax.shard_map(local, mesh=split, in_specs=in_specs, out_specs=P(grp, slab), check_vma=False)
```

time: 269 us -> 111 us (0.41)
  waiting for transfers between devices: 231 us -> 16.3 us
  starting transfers between devices: 7.08 us -> 51.9 us
  blocking collectives: 0 us -> 31.1 us
  between operations: 13.4 us -> 0.27 us
  local copies, waits for them, and re-layouts: 8.99 us -> 0.86 us
  Pallas kernels: 0 us -> 6.64 us
  matrix products: 6.5 us -> 0 us
    reduce_scatter x1 -> x0, waiting for transfers between devices: 87.2 us -> none  [local(): lax.psum_scatter(block_gemm(regrouped, masked), 'grp', scatter_dimension=...]
    all_gather x1 -> x0, waiting for transfers between devices: 80.7 us -> none  [local(): full_rows = lax.all_gather(amplitudes, 'slab', axis=1, tiled=True)]
    all_to_all x1 -> x0, waiting for transfers between devices: 62.5 us -> none  [local(): lax.all_to_all(full_rows, 'grp', split_axis=1, concat_axis=0, tiled=True)]
    ppermute x0 -> x15, starting transfers between devices: none -> 51.9 us  [the longest x2 11.5 us: local(): lax.ppermute(part, AXES, home(k, 0))]
    all_gather x0 -> x1, blocking collectives: none -> 31.1 us  [local(): here = lax.all_gather(amplitudes, 'z', axis=0, axis_index_groups=FAR_PLANES)]
    ppermute x0 -> x15, waiting for transfers between devices: none -> 16.3 us  [the longest x1 10.2 us: local(): b2 = lax.ppermute(b0, 'y', ring(NY, 2))]
    all_to_all x1 -> x0, starting transfers between devices: 7.03 us -> none  [local(): lax.all_to_all(full_rows, 'grp', split_axis=1, concat_axis=0, tiled=True)]
    pallas_call x0 -> x2, Pallas kernels: none -> 6.64 us  [gemm(): pl.pallas_call(gemm_kernel, out_shape=[jax.ShapeDtypeStruct((rows, column...]
  transfers between devices with their start and end apart: 3 -> 15, of which waited for: 3 -> 3; matrix products, arithmetic and copies ran while one was open for 0% -> 1% of each run, Pallas kernels for 0% -> 6%
where the time goes in v3:
time: 111 us; the launch traced here: 109 us
  starting transfers between devices  51.9 us (47%)
  blocking collectives  31.1 us (28%)
  waiting for transfers between devices  16.3 us (15%)
  Pallas kernels  6.64 us (6%)
  other arithmetic  2.01 us (2%)
    all_gather x1, blocking collectives, local(): here = lax.all_gather(amplitudes, 'z', axis=0, axis_index_groups=FAR_PLANES)  31.1 us
    ppermute x2, starting transfers between devices, local(): lax.ppermute(part, AXES, home(k, 0))  11.5 us
    ppermute x1, waiting for transfers between devices, local(): b2 = lax.ppermute(b0, 'y', ring(NY, 2))  10.2 us
    ppermute x4, starting transfers between devices, local(): peer_bs = [lax.ppermute(b, 'c', ring(NC, 1)) for b in bs]  8.94 us
    ppermute x2, starting transfers between devices, local(): a = [lax.ppermute(both, AXES, spread(k)) for k in range(2)]  8.33 us
    pallas_call x2, Pallas kernels, gemm(): pl.pallas_call(gemm_kernel, out_shape=[jax.ShapeDtypeStruct((rows, column...  6.64 us
    ppermute x1, starting transfers between devices, local(): there = lax.ppermute(here, 'c', ring(NC, 1))  6.48 us
    ppermute x2, waiting for transfers between devices, local(): lax.ppermute(part, AXES, home(k, 1))  6.02 us
  transfers between devices with their start and end apart: 15, of which 3 were waited for; matrix products, arithmetic and copies ran while one was open for 1% of the time, Pallas kernels for 6%

profile of v3, /device:TPU:1, one launch (start us, length us, event | category | flops | bytes accessed | tf_op | source)
XLA Modules:
  0.0 109.0 jit_solution(6825642322727421819)
XLA Ops:
  0.0 5.5 %collective-permute-start = (bf16[512,1024]{1,0:T(8,128)(2,1)}, bf16[512,1024]{1,0:T(8,128)(2,1)}, u32[]{:S(2)}, u32[]{:S(2)}) collective-permute-start(bf16[512,1024]{1,0:T(8,128)(2,1)} %bitcast.6), channel_id=1, source_target_pairs={{0,384},{128,0},{256,128},{384,256},{1,385},{129,1},{257,129},{385... | collective-permute-start | bytes 3145736 | tf_op jit(solution)/shard_map/ppermute | solution.py:104
  5.5 1.9 %collective-permute-start.1 = (bf16[512,1024]{1,0:T(8,128)(2,1)}, bf16[512,1024]{1,0:T(8,128)(2,1)}, u32[]{:S(2)}, u32[]{:S(2)}) collective-permute-start(bf16[512,1024]{1,0:T(8,128)(2,1)} %bitcast.7), channel_id=1, source_target_pairs={{0,128},{128,256},{256,384},{384,0},{1,129},{129,257},{257,385},{3... | collective-permute-start | bytes 3145736 | tf_op jit(solution)/shard_map/ppermute | solution.py:105
  7.4 31.1 %all-gather = bf16[512,512]{1,0:T(8,128)(2,1)S(1)} all-gather(bf16[128,512]{1,0:T(8,128)(2,1)} %param.4), channel_id=2, replica_groups={{0,8,16,24},{2,10,18,26},{4,12,20,28},{6,14,22,30},{1,9,17,25},{3,11,19..., dimensions={0}, use_global_device_ids=true | all-gather | bytes 655360 | tf_op jit(solution)/shard_map/all_gather | solution.py:107
  38.5 0.0 collective-permute-done.b1
  38.5 0.0 collective-permute-done.1.b3
  38.5 6.5 %collective-permute-start.2 = (bf16[4,128,512]{2,1,0:T(8,128)(2,1)S(1)}, bf16[4,128,512]{2,1,0:T(8,128)(2,1)S(1)}, u32[]{:S(2)}, u32[]{:S(2)}) collective-permute-start(bf16[4,128,512]{2,1,0:T(8,128)(2,1)S(1)} %bitcast.11), channel_id=1, source_target_pairs={{0,1},{1,0},{2,3},{3,2},{4,5},{5,4},{6,7},{7,6},{8,9},{9,8},{10,11... | collective-permute-start | bytes 1572872 | tf_op jit(solution)/shard_map/ppermute | solution.py:110
  45.0 1.9 %collective-permute-start.5 = (bf16[512,1024]{1,0:T(8,128)(2,1)}, bf16[512,1024]{1,0:T(8,128)(2,1)}, u32[]{:S(2)}, u32[]{:S(2)}) collective-permute-start(bf16[512,1024]{1,0:T(8,128)(2,1)} %bitcast.8), channel_id=1, source_target_pairs={{0,256},{128,384},{256,0},{384,128},{1,257},{129,385},{257,1},{385... | collective-permute-start | bytes 3145736 | tf_op jit(solution)/shard_map/ppermute | solution.py:109
  46.9 0.0 collective-permute-done.2
  46.9 0.0 copy-start.2
  46.9 0.0 copy-start
  46.9 1.2 %maximum_select_fusion = bf16[2,4,128,512]{3,2,1,0:T(8,128)(2,1)} fusion(bf16[1,4,128,512]{3,2,1,0:T(8,128)(2,1)S(1)} %bitcast.13, bf16[1,4,128,512]{3,2,1,0:T(8,128)(2,1)S(1)} %bitcast.12, pred[]{:T(512)S(6)} %eq.3), kind=kLoop, calls=%fused_computation | loop fusion | flops 1572864 | bytes 2097153 | tf_op jit(solution)/shard_map/jit(_where)/select_n | solution.py:111
  48.1 3.9 %collective-permute-start.3 = (bf16[2,4,128,512]{3,2,1,0:T(8,128)(2,1)}, bf16[2,4,128,512]{3,2,1,0:T(8,128)(2,1)S(1)}, u32[]{:S(2)}, u32[]{:S(2)}) collective-permute-start(bf16[2,4,128,512]{3,2,1,0:T(8,128)(2,1)} %maximum_select_fusion), channel_id=1, source_target_pairs={{0,0},{1,5},{2,62},{3,35},{4,68},{5,73},{6,98},{7,103},{8,8},{9,13... | collective-permute-start | bytes 3145736 | tf_op jit(solution)/shard_map/ppermute | solution.py:113
  52.1 4.4 %collective-permute-start.4 = (bf16[2,4,128,512]{3,2,1,0:T(8,128)(2,1)}, bf16[2,4,128,512]{3,2,1,0:T(8,128)(2,1)S(1)}, u32[]{:S(2)}, u32[]{:S(2)}) collective-permute-start(bf16[2,4,128,512]{3,2,1,0:T(8,128)(2,1)} %maximum_select_fusion), channel_id=1, source_target_pairs={{0,2},{1,31},{2,32},{3,37},{4,70},{5,67},{6,100},{7,105},{8,10},{9... | collective-permute-start | bytes 3145736 | tf_op jit(solution)/shard_map/ppermute | solution.py:113
  56.5 0.0 copy-done.2
  56.5 2.4 %collective-permute-start.8 = (s32[4]{0:T(128)S(1)}, s32[4]{0:T(128)S(1)}, u32[]{:S(2)}, u32[]{:S(2)}) collective-permute-start(s32[4]{0:T(128)S(1)} %copy-done.2), channel_id=1, source_target_pairs={{0,1},{1,0},{2,3},{3,2},{4,5},{5,4},{6,7},{7,6},{8,9},{9,8},{10,11... | collective-permute-start | bytes 56 | tf_op jit(solution)/shard_map/ppermute | solution.py:117
  58.9 0.0 copy-done
  58.9 1.9 %collective-permute-start.9 = (bf16[512,1024]{1,0:T(8,128)(2,1)S(1)}, bf16[512,1024]{1,0:T(8,128)(2,1)}, u32[]{:S(2)}, u32[]{:S(2)}) collective-permute-start(bf16[512,1024]{1,0:T(8,128)(2,1)S(1)} %bitcast.9), channel_id=1, source_target_pairs={{0,1},{1,0},{2,3},{3,2},{4,5},{5,4},{6,7},{7,6},{8,9},{9,8},{10,11... | collective-permute-start | bytes 3145736 | tf_op jit(solution)/shard_map/ppermute | solution.py:116
  60.8 0.0 collective-permute-done.8
  60.8 2.4 %collective-permute-start.10 = (bf16[512,1024]{1,0:T(8,128)(2,1)}, bf16[512,1024]{1,0:T(8,128)(2,1)}, u32[]{:S(2)}, u32[]{:S(2)}) collective-permute-start(bf16[512,1024]{1,0:T(8,128)(2,1)} %collective-permute-done.b1), channel_id=1, source_target_pairs={{0,1},{1,0},{2,3},{3,2},{4,5},{5,4},{6,7},{7,6},{8,9},{9,8},{10,11... | collective-permute-start | bytes 3145736 | tf_op jit(solution)/shard_map/ppermute | solution.py:116
  63.2 10.2 %collective-permute-done.5.b2 = bf16[512,1024]{1,0:T(8,128)(2,1)} collective-permute-done((bf16[512,1024]{1,0:T(8,128)(2,1)}, bf16[512,1024]{1,0:T(8,128)(2,1)}, u32[]{:S(2)}, u32[]{:S(2)}) %collective-permute-start.5) | collective-permute-done | bytes 1048608 | tf_op jit(solution)/shard_map/ppermute | solution.py:109
  73.5 2.7 %collective-permute-start.12 = (bf16[512,1024]{1,0:T(8,128)(2,1)}, bf16[512,1024]{1,0:T(8,128)(2,1)}, u32[]{:S(2)}, u32[]{:S(2)}) collective-permute-start(bf16[512,1024]{1,0:T(8,128)(2,1)} %collective-permute-done.1.b3), channel_id=1, source_target_pairs={{0,1},{1,0},{2,3},{3,2},{4,5},{5,4},{6,7},{7,6},{8,9},{9,8},{10,11... | collective-permute-start | bytes 3145736 | tf_op jit(solution)/shard_map/ppermute | solution.py:116
  76.2 0.0 collective-permute-done.3.a0
  76.2 1.9 %collective-permute-start.11 = (bf16[512,1024]{1,0:T(8,128)(2,1)}, bf16[512,1024]{1,0:T(8,128)(2,1)}, u32[]{:S(2)}, u32[]{:S(2)}) collective-permute-start(bf16[512,1024]{1,0:T(8,128)(2,1)} %collective-permute-done.5.b2), channel_id=1, source_target_pairs={{0,1},{1,0},{2,3},{3,2},{4,5},{5,4},{6,7},{7,6},{8,9},{9,8},{10,11... | collective-permute-start | bytes 3145736 | tf_op jit(solution)/shard_map/ppermute | solution.py:116
  78.1 0.0 copy-start.1
  78.1 0.6 copy-done.1
  78.8 0.1 reshape.11
  78.9 0.1 reshape.12
  79.0 0.1 add_add_fusion
  79.0 0.0 collective-permute-done.4.a1
  79.1 3.2 %shard_map.46 = (f32[128,512]{1,0:T(8,128)S(1)}, f32[128,512]{1,0:T(8,128)S(1)}) custom-call(s32[38]{0:T(128)S(1)} %get-tuple-element.21.info, bf16[2,4,128,512]{3,2,1,0:T(8,128)(2,1)S(1)} %collective-permute-done.3.a0, bf16[2,4,128,512]{3,2,1,0:T(8,128)(2,1)S(1)} %collective-permute-done.4.a1, bf16[512,1024]{1,0:T(8,128)(2,1)S(1)} %bitcast.10, ...), custom_call_target="tpu_custom_call" | custom-call | flops 1073741824 | bytes 6291456 | tf_op jit(solution)/shard_map/pallas_call | solution.py:87
  82.2 9.6 %collective-permute-start.6 = (f32[128,512]{1,0:T(8,128)S(1)}, f32[128,512]{1,0:T(8,128)S(1)}, u32[]{:S(2)}, u32[]{:S(2)}) collective-permute-start(f32[128,512]{1,0:T(8,128)S(1)} %get-tuple-element.17), channel_id=1, source_target_pairs={{0,0},{1,65},{2,34},{3,99},{4,68},{5,5},{6,102},{7,39},{8,8},{9,73... | collective-permute-start | bytes 786440 | tf_op jit(solution)/shard_map/ppermute | solution.py:124
  91.8 0.0 collective-permute-done.9.b0
  91.9 1.9 %collective-permute-start.7 = (f32[128,512]{1,0:T(8,128)S(1)}, f32[128,512]{1,0:T(8,128)S(1)}, u32[]{:S(2)}, u32[]{:S(2)}) collective-permute-start(f32[128,512]{1,0:T(8,128)S(1)} %get-tuple-element.18), channel_id=1, source_target_pairs={{0,96},{1,33},{2,2},{3,67},{4,36},{5,101},{6,70},{7,7},{8,104},{9,... | collective-permute-start | bytes 786440 | tf_op jit(solution)/shard_map/ppermute | solution.py:124
  93.8 0.0 collective-permute-done.10.b1
  93.8 0.0 collective-permute-done.12.b3
  93.8 0.0 collective-permute-done.11.b2
  93.8 3.5 %shard_map.47 = (f32[128,512]{1,0:T(8,128)S(1)}, f32[128,512]{1,0:T(8,128)S(1)}) custom-call(s32[38]{0:T(128)S(1)} %get-tuple-element.22.info, bf16[2,4,128,512]{3,2,1,0:T(8,128)(2,1)S(1)} %collective-permute-done.3.a0, bf16[2,4,128,512]{3,2,1,0:T(8,128)(2,1)S(1)} %collective-permute-done.4.a1, bf16[512,1024]{1,0:T(8,128)(2,1)} %collective-permute-done.9.b0, ...), custom_call_target="tpu_custom_call" | custom-call | flops 1073741824 | bytes 6291456 | tf_op jit(solution)/shard_map/pallas_call | solution.py:87
  97.3 3.0 %collective-permute-start.13 = (f32[128,512]{1,0:T(8,128)S(1)}, f32[128,512]{1,0:T(8,128)S(1)}, u32[]{:S(2)}, u32[]{:S(2)}) collective-permute-start(f32[128,512]{1,0:T(8,128)S(1)} %get-tuple-element.19), channel_id=1, source_target_pairs={{0,1},{1,64},{2,35},{3,98},{4,69},{5,4},{6,103},{7,38},{8,9},{9,72... | collective-permute-start | bytes 786440 | tf_op jit(solution)/shard_map/ppermute | solution.py:125
  100.3 1.9 %collective-permute-start.14 = (f32[128,512]{1,0:T(8,128)S(1)}, f32[128,512]{1,0:T(8,128)S(1)}, u32[]{:S(2)}, u32[]{:S(2)}) collective-permute-start(f32[128,512]{1,0:T(8,128)S(1)} %get-tuple-element.20), channel_id=1, source_target_pairs={{0,97},{1,32},{2,3},{3,66},{4,37},{5,100},{6,71},{7,6},{8,105},{9,... | collective-permute-start | bytes 786440 | tf_op jit(solution)/shard_map/ppermute | solution.py:125
  102.2 0.0 collective-permute-done.6
  102.2 0.0 collective-permute-done.7
  102.2 1.3 %collective-permute-done.13 = f32[128,512]{1,0:T(8,128)S(1)} collective-permute-done((f32[128,512]{1,0:T(8,128)S(1)}, f32[128,512]{1,0:T(8,128)S(1)}, u32[]{:S(2)}, u32[]{:S(2)}) %collective-permute-start.13) | collective-permute-done | bytes 262176 | tf_op jit(solution)/shard_map/ppermute | solution.py:125
  103.6 4.7 %collective-permute-done.14 = f32[128,512]{1,0:T(8,128)S(1)} collective-permute-done((f32[128,512]{1,0:T(8,128)S(1)}, f32[128,512]{1,0:T(8,128)S(1)}, u32[]{:S(2)}, u32[]{:S(2)}) %collective-permute-start.14) | collective-permute-done | bytes 262176 | tf_op jit(solution)/shard_map/ppermute | solution.py:125
  108.2 0.7 add_convert_fusion
  (1 shorter events, 0.0 us)
Async XLA Ops:
  0.0 38.5 %collective-permute-start = (bf16[512,1024]{1,0:T(8,128)(2,1)}, bf16[512,1024]{1,0:T(8,128)(2,1)}, u32[]{:S(2)}, u32[]{:S(2)}) collective-permute-start(bf16[512,1024]{1,0:T(8,128)(2,1)} %bitcast.6), channel_id=1, source_target_pairs={{0,384},{128,0},{256,128},{384,256},{1,385},{129,1},{257,129},{385... | collective-permute-start | bytes 3145736 | tf_op jit(solution)/shard_map/ppermute | solution.py:104
  5.5 33.0 %collective-permute-start.1 = (bf16[512,1024]{1,0:T(8,128)(2,1)}, bf16[512,1024]{1,0:T(8,128)(2,1)}, u32[]{:S(2)}, u32[]{:S(2)}) collective-permute-start(bf16[512,1024]{1,0:T(8,128)(2,1)} %bitcast.7), channel_id=1, source_target_pairs={{0,128},{128,256},{256,384},{384,0},{1,129},{129,257},{257,385},{3... | collective-permute-start | bytes 3145736 | tf_op jit(solution)/shard_map/ppermute | solution.py:105
  38.5 8.4 %collective-permute-start.2 = (bf16[4,128,512]{2,1,0:T(8,128)(2,1)S(1)}, bf16[4,128,512]{2,1,0:T(8,128)(2,1)S(1)}, u32[]{:S(2)}, u32[]{:S(2)}) collective-permute-start(bf16[4,128,512]{2,1,0:T(8,128)(2,1)S(1)} %bitcast.11), channel_id=1, source_target_pairs={{0,1},{1,0},{2,3},{3,2},{4,5},{5,4},{6,7},{7,6},{8,9},{9,8},{10,11... | collective-permute-start | bytes 1572872 | tf_op jit(solution)/shard_map/ppermute | solution.py:110
  45.0 28.5 %collective-permute-start.5 = (bf16[512,1024]{1,0:T(8,128)(2,1)}, bf16[512,1024]{1,0:T(8,128)(2,1)}, u32[]{:S(2)}, u32[]{:S(2)}) collective-permute-start(bf16[512,1024]{1,0:T(8,128)(2,1)} %bitcast.8), channel_id=1, source_target_pairs={{0,256},{128,384},{256,0},{384,128},{1,257},{129,385},{257,1},{385... | collective-permute-start | bytes 3145736 | tf_op jit(solution)/shard_map/ppermute | solution.py:109
  46.9 9.6 %copy-start.2 = (s32[4]{0:T(128)S(1)}, s32[4]{0:T(128)}, u32[]{:S(2)}) copy-start(s32[4]{0:T(128)} %param.7) | copy-start | bytes 52
  46.9 12.0 %copy-start = (bf16[4,128,1024]{2,1,0:T(8,128)(2,1)S(1)}, bf16[4,128,1024]{2,1,0:T(8,128)(2,1)}, u32[]{:S(2)}) copy-start(bf16[4,128,1024]{2,1,0:T(8,128)(2,1)} %param.5) | copy-start | bytes 3145732
  48.1 28.0 %collective-permute-start.3 = (bf16[2,4,128,512]{3,2,1,0:T(8,128)(2,1)}, bf16[2,4,128,512]{3,2,1,0:T(8,128)(2,1)S(1)}, u32[]{:S(2)}, u32[]{:S(2)}) collective-permute-start(bf16[2,4,128,512]{3,2,1,0:T(8,128)(2,1)} %maximum_select_fusion), channel_id=1, source_target_pairs={{0,0},{1,5},{2,62},{3,35},{4,68},{5,73},{6,98},{7,103},{8,8},{9,13... | collective-permute-start | bytes 3145736 | tf_op jit(solution)/shard_map/ppermute | solution.py:113
  52.1 27.0 %collective-permute-start.4 = (bf16[2,4,128,512]{3,2,1,0:T(8,128)(2,1)}, bf16[2,4,128,512]{3,2,1,0:T(8,128)(2,1)S(1)}, u32[]{:S(2)}, u32[]{:S(2)}) collective-permute-start(bf16[2,4,128,512]{3,2,1,0:T(8,128)(2,1)} %maximum_select_fusion), channel_id=1, source_target_pairs={{0,2},{1,31},{2,32},{3,37},{4,70},{5,67},{6,100},{7,105},{8,10},{9... | collective-permute-start | bytes 3145736 | tf_op jit(solution)/shard_map/ppermute | solution.py:113
  56.5 4.4 %collective-permute-start.8 = (s32[4]{0:T(128)S(1)}, s32[4]{0:T(128)S(1)}, u32[]{:S(2)}, u32[]{:S(2)}) collective-permute-start(s32[4]{0:T(128)S(1)} %copy-done.2), channel_id=1, source_target_pairs={{0,1},{1,0},{2,3},{3,2},{4,5},{5,4},{6,7},{7,6},{8,9},{9,8},{10,11... | collective-permute-start | bytes 56 | tf_op jit(solution)/shard_map/ppermute | solution.py:117
  58.9 33.0 %collective-permute-start.9 = (bf16[512,1024]{1,0:T(8,128)(2,1)S(1)}, bf16[512,1024]{1,0:T(8,128)(2,1)}, u32[]{:S(2)}, u32[]{:S(2)}) collective-permute-start(bf16[512,1024]{1,0:T(8,128)(2,1)S(1)} %bitcast.9), channel_id=1, source_target_pairs={{0,1},{1,0},{2,3},{3,2},{4,5},{5,4},{6,7},{7,6},{8,9},{9,8},{10,11... | collective-permute-start | bytes 3145736 | tf_op jit(solution)/shard_map/ppermute | solution.py:116
  60.8 32.9 %collective-permute-start.10 = (bf16[512,1024]{1,0:T(8,128)(2,1)}, bf16[512,1024]{1,0:T(8,128)(2,1)}, u32[]{:S(2)}, u32[]{:S(2)}) collective-permute-start(bf16[512,1024]{1,0:T(8,128)(2,1)} %collective-permute-done.b1), channel_id=1, source_target_pairs={{0,1},{1,0},{2,3},{3,2},{4,5},{5,4},{6,7},{7,6},{8,9},{9,8},{10,11... | collective-permute-start | bytes 3145736 | tf_op jit(solution)/shard_map/ppermute | solution.py:116
  73.5 20.3 %collective-permute-start.12 = (bf16[512,1024]{1,0:T(8,128)(2,1)}, bf16[512,1024]{1,0:T(8,128)(2,1)}, u32[]{:S(2)}, u32[]{:S(2)}) collective-permute-start(bf16[512,1024]{1,0:T(8,128)(2,1)} %collective-permute-done.1.b3), channel_id=1, source_target_pairs={{0,1},{1,0},{2,3},{3,2},{4,5},{5,4},{6,7},{7,6},{8,9},{9,8},{10,11... | collective-permute-start | bytes 3145736 | tf_op jit(solution)/shard_map/ppermute | solution.py:116
  76.2 17.6 %collective-permute-start.11 = (bf16[512,1024]{1,0:T(8,128)(2,1)}, bf16[512,1024]{1,0:T(8,128)(2,1)}, u32[]{:S(2)}, u32[]{:S(2)}) collective-permute-start(bf16[512,1024]{1,0:T(8,128)(2,1)} %collective-permute-done.5.b2), channel_id=1, source_target_pairs={{0,1},{1,0},{2,3},{3,2},{4,5},{5,4},{6,7},{7,6},{8,9},{9,8},{10,11... | collective-permute-start | bytes 3145736 | tf_op jit(solution)/shard_map/ppermute | solution.py:116
  78.1 0.7 copy-start.1
  82.2 20.0 %collective-permute-start.6 = (f32[128,512]{1,0:T(8,128)S(1)}, f32[128,512]{1,0:T(8,128)S(1)}, u32[]{:S(2)}, u32[]{:S(2)}) collective-permute-start(f32[128,512]{1,0:T(8,128)S(1)} %get-tuple-element.17), channel_id=1, source_target_pairs={{0,0},{1,65},{2,34},{3,99},{4,68},{5,5},{6,102},{7,39},{8,8},{9,73... | collective-permute-start | bytes 786440 | tf_op jit(solution)/shard_map/ppermute | solution.py:124
  91.9 10.3 %collective-permute-start.7 = (f32[128,512]{1,0:T(8,128)S(1)}, f32[128,512]{1,0:T(8,128)S(1)}, u32[]{:S(2)}, u32[]{:S(2)}) collective-permute-start(f32[128,512]{1,0:T(8,128)S(1)} %get-tuple-element.18), channel_id=1, source_target_pairs={{0,96},{1,33},{2,2},{3,67},{4,36},{5,101},{6,70},{7,7},{8,104},{9,... | collective-permute-start | bytes 786440 | tf_op jit(solution)/shard_map/ppermute | solution.py:124
  97.3 6.3 %collective-permute-start.13 = (f32[128,512]{1,0:T(8,128)S(1)}, f32[128,512]{1,0:T(8,128)S(1)}, u32[]{:S(2)}, u32[]{:S(2)}) collective-permute-start(f32[128,512]{1,0:T(8,128)S(1)} %get-tuple-element.19), channel_id=1, source_target_pairs={{0,1},{1,64},{2,35},{3,98},{4,69},{5,4},{6,103},{7,38},{8,9},{9,72... | collective-permute-start | bytes 786440 | tf_op jit(solution)/shard_map/ppermute | solution.py:125
  100.3 8.0 %collective-permute-start.14 = (f32[128,512]{1,0:T(8,128)S(1)}, f32[128,512]{1,0:T(8,128)S(1)}, u32[]{:S(2)}, u32[]{:S(2)}) collective-permute-start(f32[128,512]{1,0:T(8,128)S(1)} %get-tuple-element.20), channel_id=1, source_target_pairs={{0,97},{1,32},{2,3},{3,66},{4,37},{5,100},{6,71},{7,6},{8,105},{9,... | collective-permute-start | bytes 786440 | tf_op jit(solution)/shard_map/ppermute | solution.py:125

commit v4 on v3

v4 whole, which is shorter than its diff:
```python
import jax
import jax.numpy as jnp
import numpy as np
from jax import lax
from jax.experimental import pallas as pl
from jax.experimental.pallas import tpu as pltpu
from jax.sharding import Mesh, PartitionSpec as P

BLK = 128
NY, NX, NZ, NC = 4, 4, 16, 2
AXES = ("y", "x", "z", "c")


def moves(target):
    pairs = []
    for source in np.ndindex(NY, NX, NZ, NC):
        to = target(*source)
        pairs.append((int(np.ravel_multi_index(source, (NY, NX, NZ, NC))), int(np.ravel_multi_index(to, (NY, NX, NZ, NC)))))
    return pairs


def ring(size, step):
    return [(i, (i + step) % size) for i in range(size)]


def matched(b, info, blocks_at, start, count):
    return jnp.concatenate(
        [
            jnp.concatenate(
                [
                    jnp.where(
                        info[blocks_at + k] == info[2 + s],
                        b[s * BLK : (s + 1) * BLK, k * BLK : (k + 1) * BLK],
                        jnp.zeros((BLK, BLK), b.dtype),
                    )
                    for k in range(start, start + count)
                ],
                axis=1,
            )
            for s in range(b.shape[0] // BLK)
        ]
    )


def powers_of_two(exponents):
    power = jnp.ones(exponents.shape, jnp.float32)
    for bit in range(7):
        power = jnp.where(lax.shift_right_logical(exponents, bit) & 1 == 1, power * 2.0 ** (1 << bit), power)
    return power


def encode_kernel(a, out):
    rows, width = a.shape
    values = a[...].astype(jnp.float32)
    largest = jnp.max(jnp.abs(values))
    exponents = lax.broadcasted_iota(jnp.int32, (8, 128), 1)
    exponents = jnp.minimum(exponents, 126)
    fits = powers_of_two(exponents) * largest <= 49152.0
    exponent = jnp.max(jnp.where(fits, exponents, 0))
    scale = powers_of_two(jnp.full((8, 128), exponent, jnp.int32))[:1, :1]
    out[:rows] = (values * scale).astype(out.dtype)
    out[rows:] = jnp.full((out.shape[0] - rows, width), exponent.astype(jnp.float32), jnp.float32).astype(out.dtype)


def encode(a):
    rows, width = a.shape
    vmem = pl.BlockSpec(memory_space=pltpu.VMEM)
    return pl.pallas_call(
        encode_kernel,
        out_shape=jax.ShapeDtypeStruct((rows + 8, width), jnp.bfloat16),
        in_specs=[vmem],
        out_specs=vmem,
        compiler_params=pltpu.CompilerParams(vmem_limit_bytes=8 << 20),
        cost_estimate=pl.CostEstimate(flops=4 * rows * width, bytes_accessed=4 * rows * width, transcendentals=0),
    )(a)


def decoded(a, at):
    rows = a.shape[1] - 8
    exponents = a[at, rows:].astype(jnp.float32)[:1].astype(jnp.int32)
    return a[at, :rows] * (1.0 / powers_of_two(exponents)).astype(a.dtype)


def gemm_kernel(info, a, b0, b1, b2, b3, out):
    x, y = info[0], info[1]
    rows = out.shape[1]
    slabs, blocks = b0.shape[0] // BLK, b0.shape[1] // BLK
    total = None
    for d, b in enumerate((b0, b1, b2, b3)):
        slot = lax.rem(y + d, NY)
        for half in range(2):
            pieces = []
            for g in range(NX):
                plane = lax.rem(4 * slot + x + g + NZ - 1, NZ)
                pieces.append(decoded(a, 2 * plane + half))
            part = lax.dot_general(
                jnp.concatenate(pieces),
                matched(b, info, 2 + slabs + (slot * NX + x) * blocks, half * blocks // 2, blocks // 2),
                (((1,), (1,)), ((), ())),
                preferred_element_type=jnp.float32,
            )
            total = part if total is None else total + part
    for g in range(NX):
        out[g] = total[g * rows : (g + 1) * rows]


def gemm(info, a, bs):
    rows = BLK
    columns, width = bs[0].shape
    smem, vmem = pl.BlockSpec(memory_space=pltpu.SMEM), pl.BlockSpec(memory_space=pltpu.VMEM)
    return pl.pallas_call(
        gemm_kernel,
        out_shape=jax.ShapeDtypeStruct((NX, rows, columns), jnp.float32),
        in_specs=[smem] + [vmem] * 5,
        out_specs=vmem,
        compiler_params=pltpu.CompilerParams(vmem_limit_bytes=16 << 20),
        cost_estimate=pl.CostEstimate(
            flops=8 * rows * columns * width * NY, bytes_accessed=9 << 20, transcendentals=0
        ),
    )(info, a, *bs)


def local(amplitudes, integrals, block_irrep, slab_irrep):
    y, x = lax.axis_index("y"), lax.axis_index("x")
    slabs, slab_rows, width = integrals.shape

    a = encode(amplitudes).astype(jnp.float16)
    a = lax.ppermute(a, AXES, moves(lambda y, x, z, c: (y, z % 4, (z + x - 1) % NZ, c)))

    b0 = integrals.reshape(slabs * slab_rows, width)
    bs = [b0] + [lax.ppermute(b0, "y", ring(NY, -d)) for d in range(1, 4)]

    a = lax.all_gather(a, ("z", "c"), axis=0)
    a = a.astype(jnp.bfloat16)
    info = jnp.concatenate([jnp.stack([x, y]).astype(jnp.int32), slab_irrep, block_irrep])
    parts = gemm(info, a, bs)
    return lax.all_to_all(parts, "x", split_axis=0, concat_axis=0).sum(0).astype(jnp.bfloat16)


def solution(mesh):
    split = Mesh(mesh.devices.reshape(NY, NX, NZ, NC), AXES)
    grp, slab = ("y", "x"), ("z", "c")
    in_specs = (P(grp, slab), P(slab, None, grp), P(), P(slab))
    return jax.shard_map(local, mesh=split, in_specs=in_specs, out_specs=P(grp, slab), check_vma=False)
```

time: 111 us -> 92.7 us (0.84)
  blocking collectives: 31.1 us -> 63.2 us
  starting transfers between devices: 51.9 us -> 21.5 us
  waiting for transfers between devices: 16.3 us -> 0.01 us
  Pallas kernels: 6.64 us -> 3.36 us
    ppermute x15 -> x4, starting transfers between devices: 51.9 us -> 21.5 us  [the longest x1 12 us: local(): lax.ppermute(a, AXES, moves(lambda y, x, z, c: (y, z % 4, (z + x - 1) % N...]
    all_to_all x0 -> x1, blocking collectives: none -> 17.2 us  [local(): lax.all_to_all(parts, 'x', split_axis=0, concat_axis=0).sum(0)]
    ppermute x15 -> x4, waiting for transfers between devices: 16.3 us -> 0.01 us  [the longest x3 0.01 us: local(): bs = [b0] + [lax.ppermute(b0, 'y', ring(NY, -d)) for d in range(1, 4)]]
    all_gather x1, blocking collectives: 31.1 us -> 46 us  [local(): a = lax.all_gather(a, ('z', 'c'), axis=0)]
    pallas_call x2, Pallas kernels: 6.64 us -> 3.36 us  [the longest x1 3 us: gemm(): pl.pallas_call(gemm_kernel, out_shape=jax.ShapeDtypeStruct((NX, rows, col...]
    select_n x1 -> x0, other arithmetic: 1.2 us -> none  [local(): both = jnp.where(c == 0, jnp.stack([here, there]), jnp.stack([there, here]))]
  transfers between devices with their start and end apart: 15 -> 4, of which waited for: 3 -> 0; matrix products, arithmetic and copies ran while one was open for 1% -> 2% of each run, Pallas kernels for 6% -> 0%
where the time goes in v4:
time: 92.7 us; the launch traced here: 91.7 us
  blocking collectives  63.2 us (68%)
  starting transfers between devices  21.5 us (23%)
  Pallas kernels  3.36 us (4%)
  other arithmetic  2.45 us (3%)
  local copies, waits for them, and re-layouts  1.18 us (1%)
    all_gather x1, blocking collectives, local(): a = lax.all_gather(a, ('z', 'c'), axis=0)  46 us
    all_to_all x1, blocking collectives, local(): lax.all_to_all(parts, 'x', split_axis=0, concat_axis=0).sum(0)  17.2 us
    ppermute x1, starting transfers between devices, local(): lax.ppermute(a, AXES, moves(lambda y, x, z, c: (y, z % 4, (z + x - 1) % N...  12 us
    ppermute x3, starting transfers between devices, local(): bs = [b0] + [lax.ppermute(b0, 'y', ring(NY, -d)) for d in range(1, 4)]  9.51 us
    pallas_call x1, Pallas kernels, gemm(): pl.pallas_call(gemm_kernel, out_shape=jax.ShapeDtypeStruct((NX, rows, col...  3 us
  transfers between devices with their start and end apart: 4, of which 0 were waited for; matrix products, arithmetic and copies ran while one was open for 2% of the time, Pallas kernels for 0%

profile of v4, /device:TPU:1, one launch (start us, length us, event | category | flops | bytes accessed | tf_op | source)
XLA Modules:
  0.0 91.7 jit_solution(2921292282158010846)
XLA Ops:
  0.0 0.0 copy-start.1
  0.0 0.9 copy-done.1
  0.9 0.4 shard_map.46
  1.3 12.0 %collective-permute-start = (f16[136,512]{1,0:T(8,128)(2,1)S(1)}, f16[136,512]{1,0:T(8,128)(2,1)S(1)}, u32[]{:S(2)}, u32[]{:S(2)}) collective-permute-start(f16[136,512]{1,0:T(8,128)(2,1)S(1)} %convert_element_type.9), channel_id=1, source_target_pairs={{0,30},{1,31},{2,32},{3,33},{4,66},{5,67},{6,100},{7,101},{8,6},{9... | collective-permute-start | bytes 417800 | tf_op jit(solution)/shard_map/ppermute | solution.py:128
  13.3 4.6 %collective-permute-start.1 = (bf16[512,1024]{1,0:T(8,128)(2,1)}, bf16[512,1024]{1,0:T(8,128)(2,1)S(1)}, u32[]{:S(2)}, u32[]{:S(2)}) collective-permute-start(bf16[512,1024]{1,0:T(8,128)(2,1)} %bitcast.5), channel_id=1, source_target_pairs={{0,384},{128,0},{256,128},{384,256},{1,385},{129,1},{257,129},{385... | collective-permute-start | bytes 3145736 | tf_op jit(solution)/shard_map/ppermute | solution.py:131
  17.9 2.3 %collective-permute-start.2 = (bf16[512,1024]{1,0:T(8,128)(2,1)}, bf16[512,1024]{1,0:T(8,128)(2,1)S(1)}, u32[]{:S(2)}, u32[]{:S(2)}) collective-permute-start(bf16[512,1024]{1,0:T(8,128)(2,1)} %bitcast.6), channel_id=1, source_target_pairs={{0,256},{128,384},{256,0},{384,128},{1,257},{129,385},{257,1},{385... | collective-permute-start | bytes 3145736 | tf_op jit(solution)/shard_map/ppermute | solution.py:131
  20.2 2.6 %collective-permute-start.3 = (bf16[512,1024]{1,0:T(8,128)(2,1)}, bf16[512,1024]{1,0:T(8,128)(2,1)S(1)}, u32[]{:S(2)}, u32[]{:S(2)}) collective-permute-start(bf16[512,1024]{1,0:T(8,128)(2,1)} %bitcast.7), channel_id=1, source_target_pairs={{0,128},{128,256},{256,384},{384,0},{1,129},{129,257},{257,385},{3... | collective-permute-start | bytes 3145736 | tf_op jit(solution)/shard_map/ppermute | solution.py:131
  22.8 0.8 pad_add_fusion.info
  23.6 0.0 collective-permute-done
  23.6 46.0 %all-gather.2 = f16[4352,512]{1,0:T(8,128)(2,1)S(1)} all-gather(f16[136,512]{1,0:T(8,128)(2,1)S(1)} %collective-permute-done), channel_id=2, replica_groups=mesh['y'=4,'x'=4,'z'=16,'c'=2] {'z','c'}, dimensions={0}, use_global_device_ids=true | all-gather | bytes 4595712 | tf_op jit(solution)/shard_map/all_gather | solution.py:133
  69.5 0.0 copy-start
  69.5 0.9 convert_element_type.12
  70.4 0.0 collective-permute-done.1.b1
  70.4 0.0 collective-permute-done.2.b2
  70.5 0.0 collective-permute-done.3.b3
  70.5 0.3 copy-done
  70.7 3.0 %shard_map.47 = f32[4,128,512]{2,1,0:T(8,128)S(1)} custom-call(s32[134]{0:T(256)S(1)} %pad_add_fusion.info, bf16[32,136,512]{2,1,0:T(8,128)(2,1)S(1)} %bitcast.4, bf16[512,1024]{1,0:T(8,128)(2,1)S(1)} %bitcast.8, bf16[512,1024]{1,0:T(8,128)(2,1)S(1)} %collective-permute-done.1.b1, bf16[512,1024]{1,0:T(8,128)(2,1)S(1)} %collective-permute-done.2.b2, ...), custom_call_target="tpu_custom_call" | custom-call | flops 2147483648 | bytes 9437184 | tf_op jit(solution)/shard_map/pallas_call | solution.py:111
  73.7 17.2 %all_to_all.5 = f32[4,128,512]{2,1,0:T(8,128)S(1)} all-to-all(f32[4,128,512]{2,1,0:T(8,128)S(1)} %shard_map.47), channel_id=1, replica_groups=mesh['y'=4,'x'=4,'z'=16,'c'=2] {'x'}, dimensions={0} | all-to-all | bytes 2097152 | tf_op jit(solution)/shard_map/all_to_all | solution.py:137
  91.0 0.8 reduce_sum.9
  (1 shorter events, 0.0 us)
Async XLA Ops:
  0.0 0.9 copy-start.1
  1.3 22.2 %collective-permute-start = (f16[136,512]{1,0:T(8,128)(2,1)S(1)}, f16[136,512]{1,0:T(8,128)(2,1)S(1)}, u32[]{:S(2)}, u32[]{:S(2)}) collective-permute-start(f16[136,512]{1,0:T(8,128)(2,1)S(1)} %convert_element_type.9), channel_id=1, source_target_pairs={{0,30},{1,31},{2,32},{3,33},{4,66},{5,67},{6,100},{7,101},{8,6},{9... | collective-permute-start | bytes 417800 | tf_op jit(solution)/shard_map/ppermute | solution.py:128
  13.3 57.2 %collective-permute-start.1 = (bf16[512,1024]{1,0:T(8,128)(2,1)}, bf16[512,1024]{1,0:T(8,128)(2,1)S(1)}, u32[]{:S(2)}, u32[]{:S(2)}) collective-permute-start(bf16[512,1024]{1,0:T(8,128)(2,1)} %bitcast.5), channel_id=1, source_target_pairs={{0,384},{128,0},{256,128},{384,256},{1,385},{129,1},{257,129},{385... | collective-permute-start | bytes 3145736 | tf_op jit(solution)/shard_map/ppermute | solution.py:131
  17.9 52.5 %collective-permute-start.2 = (bf16[512,1024]{1,0:T(8,128)(2,1)}, bf16[512,1024]{1,0:T(8,128)(2,1)S(1)}, u32[]{:S(2)}, u32[]{:S(2)}) collective-permute-start(bf16[512,1024]{1,0:T(8,128)(2,1)} %bitcast.6), channel_id=1, source_target_pairs={{0,256},{128,384},{256,0},{384,128},{1,257},{129,385},{257,1},{385... | collective-permute-start | bytes 3145736 | tf_op jit(solution)/shard_map/ppermute | solution.py:131
  20.2 50.3 %collective-permute-start.3 = (bf16[512,1024]{1,0:T(8,128)(2,1)}, bf16[512,1024]{1,0:T(8,128)(2,1)S(1)}, u32[]{:S(2)}, u32[]{:S(2)}) collective-permute-start(bf16[512,1024]{1,0:T(8,128)(2,1)} %bitcast.7), channel_id=1, source_target_pairs={{0,128},{128,256},{256,384},{384,0},{1,129},{129,257},{257,385},{3... | collective-permute-start | bytes 3145736 | tf_op jit(solution)/shard_map/ppermute | solution.py:131
  69.5 1.2 %copy-start = (bf16[4,128,1024]{2,1,0:T(8,128)(2,1)S(1)}, bf16[4,128,1024]{2,1,0:T(8,128)(2,1)}, u32[]{:S(2)}) copy-start(bf16[4,128,1024]{2,1,0:T(8,128)(2,1)} %param.5) | copy-start | bytes 3145732

commit v5 on v4

--- a/solution.py
+++ b/solution.py
@@ -9,6 +9,7 @@
 BLK = 128
 NY, NX, NZ, NC = 4, 4, 16, 2
 AXES = ("y", "x", "z", "c")
+FINE = 64.0
 
 
 def moves(target):
@@ -23,13 +24,13 @@
     return [(i, (i + step) % size) for i in range(size)]
 
 
-def matched(b, info, blocks_at, start, count):
+def matched(b, slab_labels, block_labels, blocks_at, start, count):
     return jnp.concatenate(
         [
             jnp.concatenate(
                 [
                     jnp.where(
-                        info[blocks_at + k] == info[2 + s],
+                        block_labels[blocks_at + k] == slab_labels[s],
                         b[s * BLK : (s + 1) * BLK, k * BLK : (k + 1) * BLK],
                         jnp.zeros((BLK, BLK), b.dtype),
                     )
@@ -81,60 +82,85 @@
     return a[at, :rows] * (1.0 / powers_of_two(exponents)).astype(a.dtype)
 
 
-def gemm_kernel(info, a, b0, b1, b2, b3, out):
-    x, y = info[0], info[1]
+def gemm_kernel(slab_labels, block_labels, a, b0, b1, b2, b3, out):
+    x, y = lax.axis_index("x"), lax.axis_index("y")
     rows = out.shape[1]
-    slabs, blocks = b0.shape[0] // BLK, b0.shape[1] // BLK
+    blocks = b0.shape[1] // BLK
     total = None
     for d, b in enumerate((b0, b1, b2, b3)):
         slot = lax.rem(y + d, NY)
         for half in range(2):
             pieces = []
             for g in range(NX):
-                plane = lax.rem(4 * slot + x + g + NZ - 1, NZ)
+                plane = 4 * slot + lax.rem(x + g, 4)
                 pieces.append(decoded(a, 2 * plane + half))
             part = lax.dot_general(
                 jnp.concatenate(pieces),
-                matched(b, info, 2 + slabs + (slot * NX + x) * blocks, half * blocks // 2, blocks // 2),
+                matched(b, slab_labels, block_labels, (slot * NX + x) * blocks, half * blocks // 2, blocks // 2),
                 (((1,), (1,)), ((), ())),
                 preferred_element_type=jnp.float32,
             )
             total = part if total is None else total + part
+    columns = total.shape[1]
     for g in range(NX):
-        out[g] = total[g * rows : (g + 1) * rows]
+        block = total[g * rows : (g + 1) * rows]
+        largest = jnp.maximum(jnp.max(jnp.abs(block), axis=1, keepdims=True), 2.0**-100)
+        exponents = jnp.floor(FINE * (14.99 - jnp.log2(largest)))
+        out[g, :, :columns] = jnp.round(block * jnp.exp2(exponents / FINE)).astype(jnp.int32).astype(jnp.int16)
+        out[g, :, columns:] = jnp.broadcast_to(exponents, (rows, BLK)).astype(jnp.int32).astype(jnp.int16)
 
 
-def gemm(info, a, bs):
+def sum_kernel(parts, out):
+    rows, columns = out.shape
+    total = jnp.zeros(out.shape, jnp.float32)
+    for g in range(NX):
+        scale = jnp.exp2(parts[g, :, columns:].astype(jnp.int32).astype(jnp.float32)[:, :1] / -FINE)
+        total += parts[g, :, :columns].astype(jnp.int32).astype(jnp.float32) * scale
+    out[...] = total.astype(out.dtype)
+
+
+def summed(parts):
+    _, rows, columns = parts.shape
+    vmem = pl.BlockSpec(memory_space=pltpu.VMEM)
+    return pl.pallas_call(
+        sum_kernel,
+        out_shape=jax.ShapeDtypeStruct((rows, columns - BLK), jnp.bfloat16),
+        in_specs=[vmem],
+        out_specs=vmem,
+        compiler_params=pltpu.CompilerParams(vmem_limit_bytes=8 << 20),
+        cost_estimate=pl.CostEstimate(flops=8 * rows * columns, bytes_accessed=10 * rows * columns, transcendentals=0),
+    )(parts)
+
+
+def gemm(slab_labels, block_labels, a, bs):
     rows = BLK
     columns, width = bs[0].shape
     smem, vmem = pl.BlockSpec(memory_space=pltpu.SMEM), pl.BlockSpec(memory_space=pltpu.VMEM)
     return pl.pallas_call(
         gemm_kernel,
-        out_shape=jax.ShapeDtypeStruct((NX, rows, columns), jnp.float32),
-        in_specs=[smem] + [vmem] * 5,
+        out_shape=jax.ShapeDtypeStruct((NX, rows, columns + BLK), jnp.int16),
+        in_specs=[smem] * 2 + [vmem] * 5,
         out_specs=vmem,
         compiler_params=pltpu.CompilerParams(vmem_limit_bytes=16 << 20),
         cost_estimate=pl.CostEstimate(
             flops=8 * rows * columns * width * NY, bytes_accessed=9 << 20, transcendentals=0
         ),
-    )(info, a, *bs)
+    )(slab_labels, block_labels, a, *bs)
 
 
 def local(amplitudes, integrals, block_irrep, slab_irrep):
-    y, x = lax.axis_index("y"), lax.axis_index("x")
     slabs, slab_rows, width = integrals.shape
 
     a = encode(amplitudes).astype(jnp.float16)
-    a = lax.ppermute(a, AXES, moves(lambda y, x, z, c: (y, z % 4, (z + x - 1) % NZ, c)))
+    a = lax.ppermute(a, AXES, moves(lambda y, x, z, c: (y, z % 4, z // 4 * 4 + (z + x) % 4, c)))
 
     b0 = integrals.reshape(slabs * slab_rows, width)
     bs = [b0] + [lax.ppermute(b0, "y", ring(NY, -d)) for d in range(1, 4)]
 
     a = lax.all_gather(a, ("z", "c"), axis=0)
     a = a.astype(jnp.bfloat16)
-    info = jnp.concatenate([jnp.stack([x, y]).astype(jnp.int32), slab_irrep, block_irrep])
-    parts = gemm(info, a, bs)
-    return lax.all_to_all(parts, "x", split_axis=0, concat_axis=0).sum(0).astype(jnp.bfloat16)
+    parts = gemm(slab_irrep, block_irrep, a, bs)
+    return summed(lax.all_to_all(parts, "x", split_axis=0, concat_axis=0))
 
 
 def solution(mesh):

time: 92.7 us -> 88.1 us (0.950)
  starting transfers between devices: 21.5 us -> 11 us
  blocking collectives: 63.2 us -> 69.2 us
  other arithmetic: 2.45 us -> 0.93 us
    ppermute x1, starting transfers between devices: 12 us -> 0.67 us  [local(): lax.ppermute(a, AXES, moves(lambda y, x, z, c: (y, z % 4, z // 4 * 4 + (z...]
    all_gather x1, blocking collectives: 46 us -> 56 us  [local(): a = lax.all_gather(a, ('z', 'c'), axis=0)]
    all_to_all x1, blocking collectives: 17.2 us -> 13.2 us  [local(): return summed(lax.all_to_all(parts, 'x', split_axis=0, concat_axis=0))]
  transfers between devices with their start and end apart: 4 -> 4, of which waited for: 0 -> 0; matrix products, arithmetic and copies ran while one was open for 2% -> 1% of each run, Pallas kernels for 0% -> 0%
where the time goes in v5:
time: 88.1 us; the launch traced here: 86.7 us
  blocking collectives  69.2 us (79%)
  starting transfers between devices  11 us (12%)
  Pallas kernels  4.28 us (5%)
  local copies, waits for them, and re-layouts  1.2 us (1%)
  other arithmetic  0.93 us (1%)
    all_gather x1, blocking collectives, local(): a = lax.all_gather(a, ('z', 'c'), axis=0)  56 us
    all_to_all x1, blocking collectives, local(): return summed(lax.all_to_all(parts, 'x', split_axis=0, concat_axis=0))  13.2 us
    ppermute x3, starting transfers between devices, local(): bs = [b0] + [lax.ppermute(b0, 'y', ring(NY, -d)) for d in range(1, 4)]  10.3 us
    pallas_call x1, Pallas kernels, gemm(): pl.pallas_call(gemm_kernel, out_shape=jax.ShapeDtypeStruct((NX, rows, col...  3.09 us
  transfers between devices with their start and end apart: 4, of which 0 were waited for; matrix products, arithmetic and copies ran while one was open for 1% of the time, Pallas kernels for 0%

profile of v5, /device:TPU:1, one launch (start us, length us, event | category | flops | bytes accessed | tf_op | source)
XLA Modules:
  0.0 86.7 jit_solution(1262760606048144047)
XLA Ops:
  0.0 0.0 copy-start.1
  0.0 0.9 %copy-done.1 = bf16[128,512]{1,0:T(8,128)(2,1)S(1)} copy-done((bf16[128,512]{1,0:T(8,128)(2,1)S(1)}, bf16[128,512]{1,0:T(8,128)(2,1)}, u32[]{:S(2)}) %copy-start.1) | copy-done | bytes 131096
  0.9 0.4 shard_map.46
  1.3 0.7 collective-permute-start
  2.0 5.5 %collective-permute-start.1 = (bf16[512,1024]{1,0:T(8,128)(2,1)}, bf16[512,1024]{1,0:T(8,128)(2,1)S(1)}, u32[]{:S(2)}, u32[]{:S(2)}) collective-permute-start(bf16[512,1024]{1,0:T(8,128)(2,1)} %bitcast.3), channel_id=1, source_target_pairs={{0,384},{128,0},{256,128},{384,256},{1,385},{129,1},{257,129},{385... | collective-permute-start | bytes 3145736 | tf_op jit(solution)/shard_map/ppermute | solution.py:158
  7.5 2.3 %collective-permute-start.2 = (bf16[512,1024]{1,0:T(8,128)(2,1)}, bf16[512,1024]{1,0:T(8,128)(2,1)S(1)}, u32[]{:S(2)}, u32[]{:S(2)}) collective-permute-start(bf16[512,1024]{1,0:T(8,128)(2,1)} %bitcast.4), channel_id=1, source_target_pairs={{0,256},{128,384},{256,0},{384,128},{1,257},{129,385},{257,1},{385... | collective-permute-start | bytes 3145736 | tf_op jit(solution)/shard_map/ppermute | solution.py:158
  9.7 2.6 %collective-permute-start.3 = (bf16[512,1024]{1,0:T(8,128)(2,1)}, bf16[512,1024]{1,0:T(8,128)(2,1)S(1)}, u32[]{:S(2)}, u32[]{:S(2)}) collective-permute-start(bf16[512,1024]{1,0:T(8,128)(2,1)} %bitcast.5), channel_id=1, source_target_pairs={{0,128},{128,256},{256,384},{384,0},{1,129},{129,257},{257,385},{3... | collective-permute-start | bytes 3145736 | tf_op jit(solution)/shard_map/ppermute | solution.py:158
  12.3 0.0 collective-permute-done
  12.4 56.0 %all-gather.2 = f16[4352,512]{1,0:T(8,128)(2,1)S(1)} all-gather(f16[136,512]{1,0:T(8,128)(2,1)S(1)} %collective-permute-done), channel_id=2, replica_groups=mesh['y'=4,'x'=4,'z'=16,'c'=2] {'z','c'}, dimensions={0}, use_global_device_ids=true | all-gather | bytes 4595712 | tf_op jit(solution)/shard_map/all_gather | solution.py:160
  68.3 0.0 copy-start
  68.3 0.0 copy-start.2
  68.3 0.0 copy-start.3
  68.4 0.9 %convert_element_type.8 = bf16[4352,512]{1,0:T(8,128)(2,1)S(1)} convert(f16[4352,512]{1,0:T(8,128)(2,1)S(1)} %all-gather.2) | non-fusion elementwise | flops 2228224 | bytes 8912896 | tf_op jit(solution)/shard_map/convert_element_type | solution.py:161
  69.3 0.0 collective-permute-done.1.b1
  69.3 0.0 collective-permute-done.2.b2
  69.3 0.0 collective-permute-done.3.b3
  69.3 0.3 copy-done
  69.6 0.0 copy-done.2
  69.6 0.0 copy-done.3
  69.6 3.1 %shard_map.47 = s16[4,128,640]{2,1,0:T(8,128)(2,1)S(1)} custom-call(s32[4]{0:T(128)S(1)} %copy-done.2, s32[128]{0:T(128)S(1)} %copy-done.3, bf16[32,136,512]{2,1,0:T(8,128)(2,1)S(1)} %bitcast.2, bf16[512,1024]{1,0:T(8,128)(2,1)S(1)} %bitcast.6, bf16[512,1024]{1,0:T(8,128)(2,1)S(1)} %collective-permute-done.1.b1, ...), custom_call_target="tpu_custom_call" | custom-call | flops 2147483648 | bytes 9437184 | tf_op jit(solution)/shard_map/pallas_call | solution.py:139
  72.7 13.2 %all_to_all.5.parts = s16[4,128,640]{2,1,0:T(8,128)(2,1)S(1)} all-to-all(s16[4,128,640]{2,1,0:T(8,128)(2,1)S(1)} %shard_map.47), channel_id=1, replica_groups=mesh['y'=4,'x'=4,'z'=16,'c'=2] {'x'}, dimensions={0} | all-to-all | bytes 1310720 | tf_op jit(solution)/shard_map/all_to_all | solution.py:163
  85.8 0.8 shard_map.48
  (1 shorter events, 0.0 us)
Async XLA Ops:
  0.0 0.9 %copy-start.1 = (bf16[128,512]{1,0:T(8,128)(2,1)S(1)}, bf16[128,512]{1,0:T(8,128)(2,1)}, u32[]{:S(2)}) copy-start(bf16[128,512]{1,0:T(8,128)(2,1)} %a.1) | copy-start | bytes 393220
  1.3 11.0 %collective-permute-start = (f16[136,512]{1,0:T(8,128)(2,1)S(1)}, f16[136,512]{1,0:T(8,128)(2,1)S(1)}, u32[]{:S(2)}, u32[]{:S(2)}) collective-permute-start(f16[136,512]{1,0:T(8,128)(2,1)S(1)} %convert_element_type.6), channel_id=1, source_target_pairs={{0,0},{1,1},{2,34},{3,35},{4,68},{5,69},{6,102},{7,103},{8,8},{9,9... | collective-permute-start | bytes 417800 | tf_op jit(solution)/shard_map/ppermute | solution.py:155
  2.0 67.3 %collective-permute-start.1 = (bf16[512,1024]{1,0:T(8,128)(2,1)}, bf16[512,1024]{1,0:T(8,128)(2,1)S(1)}, u32[]{:S(2)}, u32[]{:S(2)}) collective-permute-start(bf16[512,1024]{1,0:T(8,128)(2,1)} %bitcast.3), channel_id=1, source_target_pairs={{0,384},{128,0},{256,128},{384,256},{1,385},{129,1},{257,129},{385... | collective-permute-start | bytes 3145736 | tf_op jit(solution)/shard_map/ppermute | solution.py:158
  7.5 61.8 %collective-permute-start.2 = (bf16[512,1024]{1,0:T(8,128)(2,1)}, bf16[512,1024]{1,0:T(8,128)(2,1)S(1)}, u32[]{:S(2)}, u32[]{:S(2)}) collective-permute-start(bf16[512,1024]{1,0:T(8,128)(2,1)} %bitcast.4), channel_id=1, source_target_pairs={{0,256},{128,384},{256,0},{384,128},{1,257},{129,385},{257,1},{385... | collective-permute-start | bytes 3145736 | tf_op jit(solution)/shard_map/ppermute | solution.py:158
  9.7 59.5 %collective-permute-start.3 = (bf16[512,1024]{1,0:T(8,128)(2,1)}, bf16[512,1024]{1,0:T(8,128)(2,1)S(1)}, u32[]{:S(2)}, u32[]{:S(2)}) collective-permute-start(bf16[512,1024]{1,0:T(8,128)(2,1)} %bitcast.5), channel_id=1, source_target_pairs={{0,128},{128,256},{256,384},{384,0},{1,129},{129,257},{257,385},{3... | collective-permute-start | bytes 3145736 | tf_op jit(solution)/shard_map/ppermute | solution.py:158
  68.3 1.2 %copy-start = (bf16[4,128,1024]{2,1,0:T(8,128)(2,1)S(1)}, bf16[4,128,1024]{2,1,0:T(8,128)(2,1)}, u32[]{:S(2)}) copy-start(bf16[4,128,1024]{2,1,0:T(8,128)(2,1)} %param.5) | copy-start | bytes 3145732
  68.3 1.2 %copy-start.2 = (s32[4]{0:T(128)S(1)}, s32[4]{0:T(128)}, u32[]{:S(2)}) copy-start(s32[4]{0:T(128)} %slab_labels.1) | copy-start | bytes 52
  68.3 1.2 %copy-start.3 = (s32[128]{0:T(128)S(1)}, s32[128]{0:T(128)}, u32[]{:S(2)}) copy-start(s32[128]{0:T(128)} %block_labels.1) | copy-start | bytes 1540

commit v6 on v5

--- a/solution.py
+++ b/solution.py
@@ -151,13 +151,12 @@
 def local(amplitudes, integrals, block_irrep, slab_irrep):
     slabs, slab_rows, width = integrals.shape
 
-    a = encode(amplitudes).astype(jnp.float16)
-    a = lax.ppermute(a, AXES, moves(lambda y, x, z, c: (y, z % 4, z // 4 * 4 + (z + x) % 4, c)))
+    a = lax.ppermute(amplitudes, AXES, moves(lambda y, x, z, c: (y, z % 4, z // 4 * 4 + (z + x) % 4, c)))
 
     b0 = integrals.reshape(slabs * slab_rows, width)
     bs = [b0] + [lax.ppermute(b0, "y", ring(NY, -d)) for d in range(1, 4)]
 
-    a = lax.all_gather(a, ("z", "c"), axis=0)
+    a = lax.all_gather(encode(a).astype(jnp.float16), ("z", "c"), axis=0)
     a = a.astype(jnp.bfloat16)
     parts = gemm(slab_irrep, block_irrep, a, bs)
     return summed(lax.all_to_all(parts, "x", split_axis=0, concat_axis=0))

time: 88.1 us -> 87.2 us (0.990)
  local copies, waits for them, and re-layouts: 1.2 us -> 0.29 us
  blocking collectives: 69.2 us -> 68.3 us
  starting transfers between devices: 11 us -> 11.9 us
    unnamed x8 -> x6, local copies, waits for them, and re-layouts: 1.2 us -> 0.29 us
where the time goes in v6:
time: 87.2 us; the launch traced here: 85.7 us
  blocking collectives  68.3 us (78%)
  starting transfers between devices  11.9 us (14%)
  Pallas kernels  4.28 us (5%)
  other arithmetic  0.93 us (1%)
    all_gather x1, blocking collectives, local(): a = lax.all_gather(encode(a).astype(jnp.float16), ('z', 'c'), axis=0)  55.1 us
    all_to_all x1, blocking collectives, local(): return summed(lax.all_to_all(parts, 'x', split_axis=0, concat_axis=0))  13.2 us
    ppermute x3, starting transfers between devices, local(): bs = [b0] + [lax.ppermute(b0, 'y', ring(NY, -d)) for d in range(1, 4)]  10.3 us
    pallas_call x1, Pallas kernels, gemm(): pl.pallas_call(gemm_kernel, out_shape=jax.ShapeDtypeStruct((NX, rows, col...  3.09 us
  transfers between devices with their start and end apart: 4, of which 0 were waited for; matrix products, arithmetic and copies ran while one was open for 1% of the time, Pallas kernels for 0%

profile of v6, /device:TPU:1, one launch (start us, length us, event | category | flops | bytes accessed | tf_op | source)
XLA Modules:
  0.0 85.7 jit_solution(11411594837017672426)
XLA Ops:
  0.0 1.6 %collective-permute-start = (bf16[128,512]{1,0:T(8,128)(2,1)}, bf16[128,512]{1,0:T(8,128)(2,1)S(1)}, u32[]{:S(2)}, u32[]{:S(2)}) collective-permute-start(bf16[128,512]{1,0:T(8,128)(2,1)} %param.4), channel_id=1, source_target_pairs={{0,0},{1,1},{2,34},{3,35},{4,68},{5,69},{6,102},{7,103},{8,8},{9,9... | collective-permute-start | bytes 393224 | tf_op jit(solution)/shard_map/ppermute | solution.py:154
  1.6 5.5 %collective-permute-start.1 = (bf16[512,1024]{1,0:T(8,128)(2,1)}, bf16[512,1024]{1,0:T(8,128)(2,1)S(1)}, u32[]{:S(2)}, u32[]{:S(2)}) collective-permute-start(bf16[512,1024]{1,0:T(8,128)(2,1)} %bitcast.3), channel_id=1, source_target_pairs={{0,384},{128,0},{256,128},{384,256},{1,385},{129,1},{257,129},{385... | collective-permute-start | bytes 3145736 | tf_op jit(solution)/shard_map/ppermute | solution.py:157
  7.0 2.3 %collective-permute-start.2 = (bf16[512,1024]{1,0:T(8,128)(2,1)}, bf16[512,1024]{1,0:T(8,128)(2,1)S(1)}, u32[]{:S(2)}, u32[]{:S(2)}) collective-permute-start(bf16[512,1024]{1,0:T(8,128)(2,1)} %bitcast.4), channel_id=1, source_target_pairs={{0,256},{128,384},{256,0},{384,128},{1,257},{129,385},{257,1},{385... | collective-permute-start | bytes 3145736 | tf_op jit(solution)/shard_map/ppermute | solution.py:157
  9.3 2.6 %collective-permute-start.3 = (bf16[512,1024]{1,0:T(8,128)(2,1)}, bf16[512,1024]{1,0:T(8,128)(2,1)S(1)}, u32[]{:S(2)}, u32[]{:S(2)}) collective-permute-start(bf16[512,1024]{1,0:T(8,128)(2,1)} %bitcast.5), channel_id=1, source_target_pairs={{0,128},{128,256},{256,384},{384,0},{1,129},{129,257},{257,385},{3... | collective-permute-start | bytes 3145736 | tf_op jit(solution)/shard_map/ppermute | solution.py:157
  11.9 0.0 collective-permute-done.a
  11.9 0.4 shard_map.46
  12.3 55.1 %all-gather.2 = f16[4352,512]{1,0:T(8,128)(2,1)S(1)} all-gather(f16[136,512]{1,0:T(8,128)(2,1)S(1)} %convert_element_type.6), channel_id=2, replica_groups=mesh['y'=4,'x'=4,'z'=16,'c'=2] {'z','c'}, dimensions={0}, use_global_device_ids=true | all-gather | bytes 4595712 | tf_op jit(solution)/shard_map/all_gather | solution.py:159
  67.4 0.0 copy-start
  67.4 0.0 copy-start.1
  67.4 0.0 copy-start.2
  67.4 0.9 %convert_element_type.8 = bf16[4352,512]{1,0:T(8,128)(2,1)S(1)} convert(f16[4352,512]{1,0:T(8,128)(2,1)S(1)} %all-gather.2) | non-fusion elementwise | flops 2228224 | bytes 8912896 | tf_op jit(solution)/shard_map/convert_element_type | solution.py:160
  68.3 0.0 collective-permute-done.1.b1
  68.4 0.0 collective-permute-done.2.b2
  68.4 0.0 collective-permute-done.3.b3
  68.4 0.3 copy-done
  68.7 0.0 copy-done.1
  68.7 0.0 copy-done.2
  68.7 3.1 %shard_map.47 = s16[4,128,640]{2,1,0:T(8,128)(2,1)S(1)} custom-call(s32[4]{0:T(128)S(1)} %copy-done.1, s32[128]{0:T(128)S(1)} %copy-done.2, bf16[32,136,512]{2,1,0:T(8,128)(2,1)S(1)} %bitcast.2, bf16[512,1024]{1,0:T(8,128)(2,1)S(1)} %bitcast.6, bf16[512,1024]{1,0:T(8,128)(2,1)S(1)} %collective-permute-done.1.b1, ...), custom_call_target="tpu_custom_call" | custom-call | flops 2147483648 | bytes 9437184 | tf_op jit(solution)/shard_map/pallas_call | solution.py:139
  71.8 13.2 %all_to_all.5.parts = s16[4,128,640]{2,1,0:T(8,128)(2,1)S(1)} all-to-all(s16[4,128,640]{2,1,0:T(8,128)(2,1)S(1)} %shard_map.47), channel_id=1, replica_groups=mesh['y'=4,'x'=4,'z'=16,'c'=2] {'x'}, dimensions={0} | all-to-all | bytes 1310720 | tf_op jit(solution)/shard_map/all_to_all | solution.py:162
  84.9 0.8 shard_map.48
  (1 shorter events, 0.0 us)
Async XLA Ops:
  0.0 11.9 %collective-permute-start = (bf16[128,512]{1,0:T(8,128)(2,1)}, bf16[128,512]{1,0:T(8,128)(2,1)S(1)}, u32[]{:S(2)}, u32[]{:S(2)}) collective-permute-start(bf16[128,512]{1,0:T(8,128)(2,1)} %param.4), channel_id=1, source_target_pairs={{0,0},{1,1},{2,34},{3,35},{4,68},{5,69},{6,102},{7,103},{8,8},{9,9... | collective-permute-start | bytes 393224 | tf_op jit(solution)/shard_map/ppermute | solution.py:154
  1.6 66.8 %collective-permute-start.1 = (bf16[512,1024]{1,0:T(8,128)(2,1)}, bf16[512,1024]{1,0:T(8,128)(2,1)S(1)}, u32[]{:S(2)}, u32[]{:S(2)}) collective-permute-start(bf16[512,1024]{1,0:T(8,128)(2,1)} %bitcast.3), channel_id=1, source_target_pairs={{0,384},{128,0},{256,128},{384,256},{1,385},{129,1},{257,129},{385... | collective-permute-start | bytes 3145736 | tf_op jit(solution)/shard_map/ppermute | solution.py:157
  7.0 61.3 %collective-permute-start.2 = (bf16[512,1024]{1,0:T(8,128)(2,1)}, bf16[512,1024]{1,0:T(8,128)(2,1)S(1)}, u32[]{:S(2)}, u32[]{:S(2)}) collective-permute-start(bf16[512,1024]{1,0:T(8,128)(2,1)} %bitcast.4), channel_id=1, source_target_pairs={{0,256},{128,384},{256,0},{384,128},{1,257},{129,385},{257,1},{385... | collective-permute-start | bytes 3145736 | tf_op jit(solution)/shard_map/ppermute | solution.py:157
  9.3 59.1 %collective-permute-start.3 = (bf16[512,1024]{1,0:T(8,128)(2,1)}, bf16[512,1024]{1,0:T(8,128)(2,1)S(1)}, u32[]{:S(2)}, u32[]{:S(2)}) collective-permute-start(bf16[512,1024]{1,0:T(8,128)(2,1)} %bitcast.5), channel_id=1, source_target_pairs={{0,128},{128,256},{256,384},{384,0},{1,129},{129,257},{257,385},{3... | collective-permute-start | bytes 3145736 | tf_op jit(solution)/shard_map/ppermute | solution.py:157
  67.4 1.2 %copy-start = (bf16[4,128,1024]{2,1,0:T(8,128)(2,1)S(1)}, bf16[4,128,1024]{2,1,0:T(8,128)(2,1)}, u32[]{:S(2)}) copy-start(bf16[4,128,1024]{2,1,0:T(8,128)(2,1)} %param.5) | copy-start | bytes 3145732
  67.4 1.2 %copy-start.1 = (s32[4]{0:T(128)S(1)}, s32[4]{0:T(128)}, u32[]{:S(2)}) copy-start(s32[4]{0:T(128)} %slab_labels.1) | copy-start | bytes 52
  67.4 1.2 %copy-start.2 = (s32[128]{0:T(128)S(1)}, s32[128]{0:T(128)}, u32[]{:S(2)}) copy-start(s32[128]{0:T(128)} %block_labels.1) | copy-start | bytes 1540

commit v7 on v6

--- a/solution.py
+++ b/solution.py
@@ -154,7 +154,8 @@
     a = lax.ppermute(amplitudes, AXES, moves(lambda y, x, z, c: (y, z % 4, z // 4 * 4 + (z + x) % 4, c)))
 
     b0 = integrals.reshape(slabs * slab_rows, width)
-    bs = [b0] + [lax.ppermute(b0, "y", ring(NY, -d)) for d in range(1, 4)]
+    b2, b1, b3 = (lax.ppermute(b0, "y", ring(NY, -d)) for d in (2, 1, 3))
+    bs = [b0, b1, b2, b3]
 
     a = lax.all_gather(encode(a).astype(jnp.float16), ("z", "c"), axis=0)
     a = a.astype(jnp.bfloat16)

time: 87.2 us -> 87.2 us (level)
  no operation moved by 1% of the time
where the time goes in v7:
time: 87.2 us; the launch traced here: 85.7 us
  blocking collectives  68.3 us (78%)
  starting transfers between devices  11.9 us (14%)
  Pallas kernels  4.28 us (5%)
  other arithmetic  0.93 us (1%)
    all_gather x1, blocking collectives, local(): a = lax.all_gather(encode(a).astype(jnp.float16), ('z', 'c'), axis=0)  55.1 us
    all_to_all x1, blocking collectives, local(): return summed(lax.all_to_all(parts, 'x', split_axis=0, concat_axis=0))  13.2 us
    ppermute x3, starting transfers between devices, local(): b2, b1, b3 = (lax.ppermute(b0, 'y', ring(NY, -d)) for d in (2, 1, 3))  10.3 us
    pallas_call x1, Pallas kernels, gemm(): pl.pallas_call(gemm_kernel, out_shape=jax.ShapeDtypeStruct((NX, rows, col...  3.09 us
  transfers between devices with their start and end apart: 4, of which 0 were waited for; matrix products, arithmetic and copies ran while one was open for 1% of the time, Pallas kernels for 0%

profile of v7, /device:TPU:1, one launch (start us, length us, event | category | flops | bytes accessed | tf_op | source)
XLA Modules:
  0.0 85.7 jit_solution(11411594837017672426)
XLA Ops:
  0.0 1.6 %collective-permute-start = (bf16[128,512]{1,0:T(8,128)(2,1)}, bf16[128,512]{1,0:T(8,128)(2,1)S(1)}, u32[]{:S(2)}, u32[]{:S(2)}) collective-permute-start(bf16[128,512]{1,0:T(8,128)(2,1)} %param.4), channel_id=1, source_target_pairs={{0,0},{1,1},{2,34},{3,35},{4,68},{5,69},{6,102},{7,103},{8,8},{9,9... | collective-permute-start | bytes 393224 | tf_op jit(solution)/shard_map/ppermute | solution.py:154
  1.6 5.5 %collective-permute-start.1 = (bf16[512,1024]{1,0:T(8,128)(2,1)}, bf16[512,1024]{1,0:T(8,128)(2,1)S(1)}, u32[]{:S(2)}, u32[]{:S(2)}) collective-permute-start(bf16[512,1024]{1,0:T(8,128)(2,1)} %bitcast.3), channel_id=1, source_target_pairs={{0,384},{128,0},{256,128},{384,256},{1,385},{129,1},{257,129},{385... | collective-permute-start | bytes 3145736 | tf_op jit(solution)/shard_map/ppermute | solution.py:157
  7.0 2.3 %collective-permute-start.2 = (bf16[512,1024]{1,0:T(8,128)(2,1)}, bf16[512,1024]{1,0:T(8,128)(2,1)S(1)}, u32[]{:S(2)}, u32[]{:S(2)}) collective-permute-start(bf16[512,1024]{1,0:T(8,128)(2,1)} %bitcast.4), channel_id=1, source_target_pairs={{0,256},{128,384},{256,0},{384,128},{1,257},{129,385},{257,1},{385... | collective-permute-start | bytes 3145736 | tf_op jit(solution)/shard_map/ppermute | solution.py:157
  9.3 2.6 %collective-permute-start.3 = (bf16[512,1024]{1,0:T(8,128)(2,1)}, bf16[512,1024]{1,0:T(8,128)(2,1)S(1)}, u32[]{:S(2)}, u32[]{:S(2)}) collective-permute-start(bf16[512,1024]{1,0:T(8,128)(2,1)} %bitcast.5), channel_id=1, source_target_pairs={{0,128},{128,256},{256,384},{384,0},{1,129},{129,257},{257,385},{3... | collective-permute-start | bytes 3145736 | tf_op jit(solution)/shard_map/ppermute | solution.py:157
  11.9 0.0 collective-permute-done.a
  11.9 0.4 shard_map.46
  12.3 55.1 %all-gather.2 = f16[4352,512]{1,0:T(8,128)(2,1)S(1)} all-gather(f16[136,512]{1,0:T(8,128)(2,1)S(1)} %convert_element_type.6), channel_id=2, replica_groups=mesh['y'=4,'x'=4,'z'=16,'c'=2] {'z','c'}, dimensions={0}, use_global_device_ids=true | all-gather | bytes 4595712 | tf_op jit(solution)/shard_map/all_gather | solution.py:160
  67.4 0.0 copy-start
  67.4 0.0 copy-start.1
  67.4 0.0 copy-start.2
  67.4 0.9 %convert_element_type.8 = bf16[4352,512]{1,0:T(8,128)(2,1)S(1)} convert(f16[4352,512]{1,0:T(8,128)(2,1)S(1)} %all-gather.2) | non-fusion elementwise | flops 2228224 | bytes 8912896 | tf_op jit(solution)/shard_map/convert_element_type | solution.py:161
  68.3 0.0 collective-permute-done.1.b1
  68.4 0.0 collective-permute-done.2.b2
  68.4 0.0 collective-permute-done.3.b3
  68.4 0.3 copy-done
  68.7 0.0 copy-done.1
  68.7 0.0 copy-done.2
  68.7 3.1 %shard_map.47 = s16[4,128,640]{2,1,0:T(8,128)(2,1)S(1)} custom-call(s32[4]{0:T(128)S(1)} %copy-done.1, s32[128]{0:T(128)S(1)} %copy-done.2, bf16[32,136,512]{2,1,0:T(8,128)(2,1)S(1)} %bitcast.2, bf16[512,1024]{1,0:T(8,128)(2,1)S(1)} %bitcast.6, bf16[512,1024]{1,0:T(8,128)(2,1)S(1)} %collective-permute-done.1.b1, ...), custom_call_target="tpu_custom_call" | custom-call | flops 2147483648 | bytes 9437184 | tf_op jit(solution)/shard_map/pallas_call | solution.py:139
  71.8 13.2 %all_to_all.5.parts = s16[4,128,640]{2,1,0:T(8,128)(2,1)S(1)} all-to-all(s16[4,128,640]{2,1,0:T(8,128)(2,1)S(1)} %shard_map.47), channel_id=1, replica_groups=mesh['y'=4,'x'=4,'z'=16,'c'=2] {'x'}, dimensions={0} | all-to-all | bytes 1310720 | tf_op jit(solution)/shard_map/all_to_all | solution.py:163
  84.9 0.8 shard_map.48
  (1 shorter events, 0.0 us)
Async XLA Ops:
  0.0 11.9 %collective-permute-start = (bf16[128,512]{1,0:T(8,128)(2,1)}, bf16[128,512]{1,0:T(8,128)(2,1)S(1)}, u32[]{:S(2)}, u32[]{:S(2)}) collective-permute-start(bf16[128,512]{1,0:T(8,128)(2,1)} %param.4), channel_id=1, source_target_pairs={{0,0},{1,1},{2,34},{3,35},{4,68},{5,69},{6,102},{7,103},{8,8},{9,9... | collective-permute-start | bytes 393224 | tf_op jit(solution)/shard_map/ppermute | solution.py:154
  1.6 66.8 %collective-permute-start.1 = (bf16[512,1024]{1,0:T(8,128)(2,1)}, bf16[512,1024]{1,0:T(8,128)(2,1)S(1)}, u32[]{:S(2)}, u32[]{:S(2)}) collective-permute-start(bf16[512,1024]{1,0:T(8,128)(2,1)} %bitcast.3), channel_id=1, source_target_pairs={{0,384},{128,0},{256,128},{384,256},{1,385},{129,1},{257,129},{385... | collective-permute-start | bytes 3145736 | tf_op jit(solution)/shard_map/ppermute | solution.py:157
  7.0 61.3 %collective-permute-start.2 = (bf16[512,1024]{1,0:T(8,128)(2,1)}, bf16[512,1024]{1,0:T(8,128)(2,1)S(1)}, u32[]{:S(2)}, u32[]{:S(2)}) collective-permute-start(bf16[512,1024]{1,0:T(8,128)(2,1)} %bitcast.4), channel_id=1, source_target_pairs={{0,256},{128,384},{256,0},{384,128},{1,257},{129,385},{257,1},{385... | collective-permute-start | bytes 3145736 | tf_op jit(solution)/shard_map/ppermute | solution.py:157
  9.3 59.1 %collective-permute-start.3 = (bf16[512,1024]{1,0:T(8,128)(2,1)}, bf16[512,1024]{1,0:T(8,128)(2,1)S(1)}, u32[]{:S(2)}, u32[]{:S(2)}) collective-permute-start(bf16[512,1024]{1,0:T(8,128)(2,1)} %bitcast.5), channel_id=1, source_target_pairs={{0,128},{128,256},{256,384},{384,0},{1,129},{129,257},{257,385},{3... | collective-permute-start | bytes 3145736 | tf_op jit(solution)/shard_map/ppermute | solution.py:157
  67.4 1.2 %copy-start = (bf16[4,128,1024]{2,1,0:T(8,128)(2,1)S(1)}, bf16[4,128,1024]{2,1,0:T(8,128)(2,1)}, u32[]{:S(2)}) copy-start(bf16[4,128,1024]{2,1,0:T(8,128)(2,1)} %param.5) | copy-start | bytes 3145732
  67.4 1.2 %copy-start.1 = (s32[4]{0:T(128)S(1)}, s32[4]{0:T(128)}, u32[]{:S(2)}) copy-start(s32[4]{0:T(128)} %slab_labels.1) | copy-start | bytes 52
  67.4 1.2 %copy-start.2 = (s32[128]{0:T(128)S(1)}, s32[128]{0:T(128)}, u32[]{:S(2)}) copy-start(s32[128]{0:T(128)} %block_labels.1) | copy-start | bytes 1540

commit v8 on v7

--- a/solution.py
+++ b/solution.py
@@ -154,7 +154,7 @@
     a = lax.ppermute(amplitudes, AXES, moves(lambda y, x, z, c: (y, z % 4, z // 4 * 4 + (z + x) % 4, c)))
 
     b0 = integrals.reshape(slabs * slab_rows, width)
-    b2, b1, b3 = (lax.ppermute(b0, "y", ring(NY, -d)) for d in (2, 1, 3))
+    b1, b3, b2 = (lax.ppermute(b0, "y", ring(NY, -d)) for d in (1, 3, 2))
     bs = [b0, b1, b2, b3]
 
     a = lax.all_gather(encode(a).astype(jnp.float16), ("z", "c"), axis=0)

time: 87.2 us -> 87.2 us (level)
  no operation moved by 1% of the time
where the time goes in v8:
time: 87.2 us; the launch traced here: 85.7 us
  blocking collectives  68.3 us (78%)
  starting transfers between devices  11.9 us (14%)
  Pallas kernels  4.28 us (5%)
  other arithmetic  0.93 us (1%)
    all_gather x1, blocking collectives, local(): a = lax.all_gather(encode(a).astype(jnp.float16), ('z', 'c'), axis=0)  55.1 us
    all_to_all x1, blocking collectives, local(): return summed(lax.all_to_all(parts, 'x', split_axis=0, concat_axis=0))  13.2 us
    ppermute x3, starting transfers between devices, local(): b1, b3, b2 = (lax.ppermute(b0, 'y', ring(NY, -d)) for d in (1, 3, 2))  10.3 us
    pallas_call x1, Pallas kernels, gemm(): pl.pallas_call(gemm_kernel, out_shape=jax.ShapeDtypeStruct((NX, rows, col...  3.09 us
  transfers between devices with their start and end apart: 4, of which 0 were waited for; matrix products, arithmetic and copies ran while one was open for 1% of the time, Pallas kernels for 0%

profile of v8, /device:TPU:1, one launch (start us, length us, event | category | flops | bytes accessed | tf_op | source)
XLA Modules:
  0.0 85.7 jit_solution(11411594837017672426)
XLA Ops:
  0.0 1.6 %collective-permute-start = (bf16[128,512]{1,0:T(8,128)(2,1)}, bf16[128,512]{1,0:T(8,128)(2,1)S(1)}, u32[]{:S(2)}, u32[]{:S(2)}) collective-permute-start(bf16[128,512]{1,0:T(8,128)(2,1)} %param.4), channel_id=1, source_target_pairs={{0,0},{1,1},{2,34},{3,35},{4,68},{5,69},{6,102},{7,103},{8,8},{9,9... | collective-permute-start | bytes 393224 | tf_op jit(solution)/shard_map/ppermute | solution.py:154
  1.6 5.5 %collective-permute-start.1 = (bf16[512,1024]{1,0:T(8,128)(2,1)}, bf16[512,1024]{1,0:T(8,128)(2,1)S(1)}, u32[]{:S(2)}, u32[]{:S(2)}) collective-permute-start(bf16[512,1024]{1,0:T(8,128)(2,1)} %bitcast.3), channel_id=1, source_target_pairs={{0,384},{128,0},{256,128},{384,256},{1,385},{129,1},{257,129},{385... | collective-permute-start | bytes 3145736 | tf_op jit(solution)/shard_map/ppermute | solution.py:157
  7.0 2.3 %collective-permute-start.2 = (bf16[512,1024]{1,0:T(8,128)(2,1)}, bf16[512,1024]{1,0:T(8,128)(2,1)S(1)}, u32[]{:S(2)}, u32[]{:S(2)}) collective-permute-start(bf16[512,1024]{1,0:T(8,128)(2,1)} %bitcast.4), channel_id=1, source_target_pairs={{0,256},{128,384},{256,0},{384,128},{1,257},{129,385},{257,1},{385... | collective-permute-start | bytes 3145736 | tf_op jit(solution)/shard_map/ppermute | solution.py:157
  9.3 2.6 %collective-permute-start.3 = (bf16[512,1024]{1,0:T(8,128)(2,1)}, bf16[512,1024]{1,0:T(8,128)(2,1)S(1)}, u32[]{:S(2)}, u32[]{:S(2)}) collective-permute-start(bf16[512,1024]{1,0:T(8,128)(2,1)} %bitcast.5), channel_id=1, source_target_pairs={{0,128},{128,256},{256,384},{384,0},{1,129},{129,257},{257,385},{3... | collective-permute-start | bytes 3145736 | tf_op jit(solution)/shard_map/ppermute | solution.py:157
  11.9 0.0 collective-permute-done.a
  11.9 0.4 shard_map.46
  12.3 55.1 %all-gather.2 = f16[4352,512]{1,0:T(8,128)(2,1)S(1)} all-gather(f16[136,512]{1,0:T(8,128)(2,1)S(1)} %convert_element_type.6), channel_id=2, replica_groups=mesh['y'=4,'x'=4,'z'=16,'c'=2] {'z','c'}, dimensions={0}, use_global_device_ids=true | all-gather | bytes 4595712 | tf_op jit(solution)/shard_map/all_gather | solution.py:160
  67.4 0.0 copy-start
  67.4 0.0 copy-start.1
  67.4 0.0 copy-start.2
  67.4 0.9 %convert_element_type.8 = bf16[4352,512]{1,0:T(8,128)(2,1)S(1)} convert(f16[4352,512]{1,0:T(8,128)(2,1)S(1)} %all-gather.2) | non-fusion elementwise | flops 2228224 | bytes 8912896 | tf_op jit(solution)/shard_map/convert_element_type | solution.py:161
  68.3 0.0 collective-permute-done.1.b1
  68.4 0.0 collective-permute-done.2.b2
  68.4 0.0 collective-permute-done.3.b3
  68.4 0.3 copy-done
  68.7 0.0 copy-done.1
  68.7 0.0 copy-done.2
  68.7 3.1 %shard_map.47 = s16[4,128,640]{2,1,0:T(8,128)(2,1)S(1)} custom-call(s32[4]{0:T(128)S(1)} %copy-done.1, s32[128]{0:T(128)S(1)} %copy-done.2, bf16[32,136,512]{2,1,0:T(8,128)(2,1)S(1)} %bitcast.2, bf16[512,1024]{1,0:T(8,128)(2,1)S(1)} %bitcast.6, bf16[512,1024]{1,0:T(8,128)(2,1)S(1)} %collective-permute-done.1.b1, ...), custom_call_target="tpu_custom_call" | custom-call | flops 2147483648 | bytes 9437184 | tf_op jit(solution)/shard_map/pallas_call | solution.py:139
  71.8 13.2 %all_to_all.5.parts = s16[4,128,640]{2,1,0:T(8,128)(2,1)S(1)} all-to-all(s16[4,128,640]{2,1,0:T(8,128)(2,1)S(1)} %shard_map.47), channel_id=1, replica_groups=mesh['y'=4,'x'=4,'z'=16,'c'=2] {'x'}, dimensions={0} | all-to-all | bytes 1310720 | tf_op jit(solution)/shard_map/all_to_all | solution.py:163
  84.9 0.8 shard_map.48
  (1 shorter events, 0.0 us)
Async XLA Ops:
  0.0 11.9 %collective-permute-start = (bf16[128,512]{1,0:T(8,128)(2,1)}, bf16[128,512]{1,0:T(8,128)(2,1)S(1)}, u32[]{:S(2)}, u32[]{:S(2)}) collective-permute-start(bf16[128,512]{1,0:T(8,128)(2,1)} %param.4), channel_id=1, source_target_pairs={{0,0},{1,1},{2,34},{3,35},{4,68},{5,69},{6,102},{7,103},{8,8},{9,9... | collective-permute-start | bytes 393224 | tf_op jit(solution)/shard_map/ppermute | solution.py:154
  1.6 66.8 %collective-permute-start.1 = (bf16[512,1024]{1,0:T(8,128)(2,1)}, bf16[512,1024]{1,0:T(8,128)(2,1)S(1)}, u32[]{:S(2)}, u32[]{:S(2)}) collective-permute-start(bf16[512,1024]{1,0:T(8,128)(2,1)} %bitcast.3), channel_id=1, source_target_pairs={{0,384},{128,0},{256,128},{384,256},{1,385},{129,1},{257,129},{385... | collective-permute-start | bytes 3145736 | tf_op jit(solution)/shard_map/ppermute | solution.py:157
  7.0 61.3 %collective-permute-start.2 = (bf16[512,1024]{1,0:T(8,128)(2,1)}, bf16[512,1024]{1,0:T(8,128)(2,1)S(1)}, u32[]{:S(2)}, u32[]{:S(2)}) collective-permute-start(bf16[512,1024]{1,0:T(8,128)(2,1)} %bitcast.4), channel_id=1, source_target_pairs={{0,256},{128,384},{256,0},{384,128},{1,257},{129,385},{257,1},{385... | collective-permute-start | bytes 3145736 | tf_op jit(solution)/shard_map/ppermute | solution.py:157
  9.3 59.1 %collective-permute-start.3 = (bf16[512,1024]{1,0:T(8,128)(2,1)}, bf16[512,1024]{1,0:T(8,128)(2,1)S(1)}, u32[]{:S(2)}, u32[]{:S(2)}) collective-permute-start(bf16[512,1024]{1,0:T(8,128)(2,1)} %bitcast.5), channel_id=1, source_target_pairs={{0,128},{128,256},{256,384},{384,0},{1,129},{129,257},{257,385},{3... | collective-permute-start | bytes 3145736 | tf_op jit(solution)/shard_map/ppermute | solution.py:157
  67.4 1.2 %copy-start = (bf16[4,128,1024]{2,1,0:T(8,128)(2,1)S(1)}, bf16[4,128,1024]{2,1,0:T(8,128)(2,1)}, u32[]{:S(2)}) copy-start(bf16[4,128,1024]{2,1,0:T(8,128)(2,1)} %param.5) | copy-start | bytes 3145732
  67.4 1.2 %copy-start.1 = (s32[4]{0:T(128)S(1)}, s32[4]{0:T(128)}, u32[]{:S(2)}) copy-start(s32[4]{0:T(128)} %slab_labels.1) | copy-start | bytes 52
  67.4 1.2 %copy-start.2 = (s32[128]{0:T(128)S(1)}, s32[128]{0:T(128)}, u32[]{:S(2)}) copy-start(s32[128]{0:T(128)} %block_labels.1) | copy-start | bytes 1540
